TPU v7x, 32 devices: a whole 2x2x4 slice. The times are simulated.
32 devices in a mesh: batch: 16 (over z, y, x), branch: 2 (over core).
Axes of the slice: x: 2, y: 2, z: 4, core: 2. Of those that a mesh axis runs over, the one named last changes fastest.
Arguments:
- inputs: bfloat16 [8192, 2048], P('batch', 'branch'), may hold values from -6 to 6
- cotangent: bfloat16 [8192, 2048], P('batch', 'branch'), may hold values from -7.2 to 7.2
- segment_ids: int32 [16, 512], P('batch'), may hold values from 0 to 2, never falling along the last dimension, each value on 1 to 256 neighbouring positions
- w_qkv: float32 [2048, 3, 2048], P('batch', None, 'branch'), may hold values from -0.125 to 0.125
- w_out: float32 [2048, 2048], P('branch', 'batch'), may hold values from -0.75 to 0.75
- w_fc1: float32 [2048, 8192], P('batch', 'branch'), may hold values from -0.125 to 0.125
- w_fc2: float32 [8192, 2048], P('branch', 'batch'), may hold values from -0.0625 to 0.0625
- norm_params: float32 [4, 2048], replicated, may hold values from -1.2 to 3.5, as said below
- proj_bias: float32 [5, 2048], P(None, 'branch'), may hold values from -4 to 4
- fc1_bias: float32 [8192], P('branch'), may hold values from -4 to 4
- qkv_rows: float32 [2048], P('batch'), may hold values from 2348810.2 to 9563013
- qkv_cols: float32 [3, 2048], P(None, 'branch'), may hold values from 838860.8 to 3187671
- out_rows: float32 [2048], P('branch'), may hold values from 72142.03 to 285212.7
- out_cols: float32 [2048], P('batch'), may hold values from 72142.03 to 285212.7
- fc1_rows: float32 [2048], P('batch'), may hold values from 1677721.6 to 6710886.5
- fc1_cols: float32 [8192], P('branch'), may hold values from 419430.4 to 1677721.6
- fc2_rows: float32 [8192], P('branch'), may hold values from 1140850.8 to 4529848.5
- fc2_cols: float32 [2048], P('batch'), may hold values from 4563403 to 18119394
- norm_second: float32 [4, 2048], replicated, may hold values from 1556.48 to 6225.92
- bias_second: float32 [5, 2048], P(None, 'branch'), may hold values from 1556.48 to 6225.92
- fc1b_second: float32 [8192], P('branch'), may hold values from 163.84 to 655.36
Outputs:
- output: bfloat16 [8192, 2048], P('batch', 'branch')
- input_grad: bfloat16 [8192, 2048], P('batch', 'branch')
- qkv_grad: float32 [2048, 3, 2048], P('batch', None, 'branch')
- qkv_weight: float32 [2048, 3, 2048], P('batch', None, 'branch')
- qkv_row_stat: float32 [2048], P('batch')
- qkv_col_stat: float32 [3, 2048], P(None, 'branch')
- qkv_copy: bfloat16 [2048, 3, 2048], P('batch', None, 'branch')
- out_grad: float32 [2048, 2048], P('branch', 'batch')
- out_weight: float32 [2048, 2048], P('branch', 'batch')
- out_row_stat: float32 [2048], P('branch')
- out_col_stat: float32 [2048], P('batch')
- out_copy: bfloat16 [2048, 2048], P('branch', 'batch')
- fc1_grad: float32 [2048, 8192], P('batch', 'branch')
- fc1_weight: float32 [2048, 8192], P('batch', 'branch')
- fc1_row_stat: float32 [2048], P('batch')
- fc1_col_stat: float32 [8192], P('branch')
- fc1_copy: bfloat16 [2048, 8192], P('batch', 'branch')
- fc2_grad: float32 [8192, 2048], P('branch', 'batch')
- fc2_weight: float32 [8192, 2048], P('branch', 'batch')
- fc2_row_stat: float32 [8192], P('branch')
- fc2_col_stat: float32 [2048], P('batch')
- fc2_copy: bfloat16 [8192, 2048], P('branch', 'batch')
- norm_grad: float32 [4, 2048], replicated
- norm_moment: float32 [4, 2048], replicated
- norm_new: float32 [4, 2048], replicated
- bias_grad: float32 [5, 2048], P(None, 'branch')
- bias_moment: float32 [5, 2048], P(None, 'branch')
- bias_new: float32 [5, 2048], P(None, 'branch')
- fc1b_grad: float32 [8192], P('branch')
- fc1b_moment: float32 [8192], P('branch')
- fc1b_new: float32 [8192], P('branch')
Inputs may be any that keep to these rules, and one draw needn't show every extreme that they name: `segment_ids`: within each pack the ids never fall, each of the 3 ids is present, and one id holds exactly 256 positions, none more. `norm_params`: rows 0 and 2 are positive.
All inputs are finite; a program needn't handle non-finite values.
Results may differ from a plain program's by a relative error of at most 0.0065.
The roundings to bfloat16 on the way count: a program that leaves them out, or rounds other values in their place, can miss the bound.
Values may be sent and summed in bfloat16 or wider, within the bound.
A program may use at most 320 MiB of HBM per device.

v0:
```python
import functools

import jax
import jax.numpy as jnp
from jax import lax
from jax.experimental import pallas as pl
from jax.experimental.pallas import tpu as pltpu
from jax.sharding import PartitionSpec as P

D = 2048
HD = 128
ROT = 32
FF = 8192
STEP = 10


EPS_NORM = 1e-05
EPS_SQUARE = 1e-30
RATE = 0.3
FLOOR_RATE = 0.001


def decay_rate():
    return 1.0 - STEP ** (-0.8)


def squares(gradient):
    return gradient * gradient + EPS_SQUARE


def renew_stat(old_stat, new_sum):
    decay = decay_rate()
    return decay * old_stat + (1.0 - decay) * new_sum


def second_step(gradient, second):
    second_new = renew_stat(second, squares(gradient))
    return (second_new, gradient * lax.rsqrt(second_new))


INNER = 4
HEADS_DEV = 2
CUTS = 4
CHUNKS = HEADS_DEV + CUTS
CUT = 256
WIDE = 512
MESH = pl.DeviceIdType.MESH


def flip(index, step):
    return index + step * (1 - 2 * lax.rem(index // step, 2))


def nn(left, right):
    return jnp.dot(left, right, preferred_element_type=jnp.float32)


def nt(left, right):
    return lax.dot_general(
        left, right, (((1,), (1,)), ((), ())), preferred_element_type=jnp.float32
    )


def tn(left, right):
    return lax.dot_general(
        left, right, (((0,), (0,)), ((), ())), preferred_element_type=jnp.float32
    )


def block_kernel(
    count,
    wst,
    xin,
    yin,
    turn_ref,
    norm_ref,
    bias_h,
    bias_f,
    gr,
    xr,
    xo,
    qb,
    fb,
    cs,
    st,
    H1,
    H2,
    DY,
    W,
    TA,
    G,
    sbuf,
    fbuf,
    rsb,
    sib_send,
    sib_land,
    psend,
    own,
    a2a_s,
    a2a_r,
    loc_s,
    ag_s,
    ag_r,
    x_s,
    x_r,
    sx_s,
    sx_r,
    rs_s,
    rs_r,
    gr_s,
    gr_r,
    sib_s,
    sib_r,
    p_s,
    p_r,
    tmp_s,
    free_s,
):
    outer = count // INNER
    S = outer - 1
    T, half = xin.shape
    R = wst.shape[2]
    block = INNER * R
    QT = T // 2
    b = lax.axis_index("batch")
    c = lax.axis_index("branch")
    q = lax.rem(b, INNER)
    o = b // INNER
    bx, by = flip(b, 1), flip(b, 2)
    bxy = flip(bx, 2)
    near = (bx, by, bxy)
    da = 1 + c
    db = 2 - c
    b_first = bx * (1 - c) + by * c
    b_second = by * (1 - c) + bx * c

    def remote(src, dst, ssem, rsem, to_b, to_c):
        return pltpu.make_async_remote_copy(
            src_ref=src,
            dst_ref=dst,
            send_sem=ssem,
            recv_sem=rsem,
            device_id=(to_b, to_c),
            device_id_type=MESH,
        )

    barrier = pltpu.get_barrier_semaphore()
    for who in near:
        pl.semaphore_signal(barrier, inc=1, device_id=(who, c), device_id_type=MESH)
    pl.semaphore_signal(barrier, inc=1, device_id=(b, 1 - c), device_id_type=MESH)

    @pl.when(o > 0)
    def _():
        pl.semaphore_signal(barrier, inc=1, device_id=(b - INNER, c), device_id_type=MESH)

    @pl.when(o < outer - 1)
    def _():
        pl.semaphore_signal(barrier, inc=1, device_id=(b + INNER, c), device_id_type=MESH)

    pl.semaphore_wait(barrier, 4 + jnp.minimum(o, 1) + jnp.minimum(outer - 1 - o, 1))

    def a2a_copy(k, d, received=False):
        to = near[d - 1]
        row = (to if received else b) * R
        return remote(
            wst.at[k, lax.rem(to, INNER)],
            W.at[k, pl.ds(pl.multiple_of(row, 16), R)],
            a2a_s.at[k, d - 1],
            a2a_r.at[k, d - 1],
            to,
            c,
        )

    def a2a_local(k):
        return pltpu.make_async_copy(
            wst.at[k, q], W.at[k, pl.ds(pl.multiple_of(b * R, 16), R)], loc_s.at[k]
        )

    def a2a_start(k):
        for d in range(1, INNER):
            a2a_copy(k, d).start()
        a2a_local(k).start()

    def a2a_wait(k):
        for d in range(1, INNER):
            a2a_copy(k, d, True).wait_recv()
        a2a_local(k).wait()

    def ag_copy(k, way, s, part):
        rows = pl.ds(pl.multiple_of(part * block, 16), block)
        to = b + INNER if way == 0 else b - INNER
        return remote(
            W.at[k, rows], W.at[k, rows], ag_s.at[k, way, s - 1], ag_r.at[k, way, s - 1], to, c
        )

    def ag_sends(k, s, what):
        @pl.when((o >= s - 1) & (o <= outer - 2))
        def _():
            what(ag_copy(k, 0, s, o - s + 1))

        @pl.when((o >= 1) & (o <= outer - s))
        def _():
            what(ag_copy(k, 1, s, o + s - 1))

    def ag_wait(k, s):
        @pl.when(o >= s)
        def _():
            ag_copy(k, 0, s, o - s).wait_recv()

        @pl.when(o <= outer - 1 - s)
        def _():
            ag_copy(k, 1, s, o + s).wait_recv()

    def ag_range(low, high):
        def step(n, carry):
            k = n // S
            s = lax.rem(n, S) + 1

            @pl.when(s == 1)
            def _():
                a2a_wait(k)

            @pl.when(s > 1)
            def _():
                ag_wait(k, s - 1)

            ag_sends(k, s, lambda copy: copy.start())
            return carry

        lax.fori_loop(low, high, step, 0)

    def ag(low, high):
        ag_range(low * S // 3, high * S // 3)

    def spot(buf, slot):
        return buf.at[
            pl.ds(pl.multiple_of(slot * T, 16), T), pl.ds(pl.multiple_of(c * half, 128), half)
        ]

    def other_spot(buf, slot):
        return buf.at[
            pl.ds(pl.multiple_of(slot * T, 16), T), pl.ds(pl.multiple_of((1 - c) * half, 128), half)
        ]

    def sx_copy(i, buf, slot, src=None):
        place = spot(buf, slot)
        return remote(place if src is None else src, place, sx_s.at[i, slot], sx_r.at[i, slot], b, 1 - c)

    def sx_wait(i, buf, slot):
        remote(
            other_spot(buf, slot), other_spot(buf, slot), sx_s.at[i, slot], sx_r.at[i, slot], b, 1 - c
        ).wait_recv()

    def x_first(i, src, buf):
        return remote(src, spot(buf, da), x_s.at[i, da - 1], x_r.at[i, da - 1], b_first, c)

    def x_second(i, src, buf):
        return remote(src, spot(buf, db), x_s.at[i, db - 1], x_r.at[i, db - 1], b_second, c)

    def x_forward(i, buf):
        return remote(spot(buf, da), spot(buf, 3), x_s.at[i, 2], x_r.at[i, 2], b_second, c)

    def x_diag(i, buf):
        return remote(spot(buf, 3), spot(buf, 3), x_s.at[i, 2], x_r.at[i, 2], b_second, c)

    def x_local(i, src, buf):
        return pltpu.make_async_copy(src, spot(buf, 0), tmp_s.at[i])

    def gather_one(i, src, buf):
        x_first(i, src, buf).start()
        x_local(i, src, buf).start()
        sx_copy(i, buf, 0, src).start()

    def gather_two(i, src, buf):
        x_first(i, src, buf).wait_recv()
        x_second(i, src, buf).start()
        x_forward(i, buf).start()
        sx_copy(i, buf, da).start()

    def gather_three(i, src, buf):
        x_second(i, src, buf).wait_recv()
        sx_copy(i, buf, db).start()
        x_diag(i, buf).wait_recv()
        sx_copy(i, buf, 3).start()

    def gather_sent(i, src, buf):
        x_first(i, src, buf).wait_send()
        x_second(i, src, buf).wait_send()
        x_forward(i, buf).wait_send()
        sx_copy(i, buf, 0, src).wait_send()
        for slot in range(1, INNER):
            sx_copy(i, buf, slot).wait_send()

    lane_n = lax.broadcasted_iota(jnp.int32, (64, 128), 1)

    def norm_rows(slot):
        def step(i, carry):
            rows = pl.ds(pl.multiple_of(slot * T + i * 64, 64), 64)
            values = H1[rows, :].astype(jnp.float32)
            mean = jnp.mean(values, axis=-1, keepdims=True)
            centered = values - mean
            inverse = lax.rsqrt(jnp.mean(centered * centered, axis=-1, keepdims=True) + EPS_NORM)
            normed = centered * inverse
            if slot == 0:
                st[pl.ds(pl.multiple_of(i * 64, 64), 64), :] = jnp.where(lane_n == 0, mean, inverse)
            H1[rows, :] = (normed * norm_ref[0:1, :] + norm_ref[1:2, :]).astype(jnp.bfloat16)
            H2[rows, :] = (normed * norm_ref[2:3, :] + norm_ref[3:4, :]).astype(jnp.bfloat16)
            return carry

        lax.fori_loop(0, T // 64, step, 0)

    lane = lax.broadcasted_iota(jnp.int32, (T, HD), 1)
    scale = HD ** (-0.5)

    def partner(tensor):
        return jnp.where(
            lane < ROT // 2,
            pltpu.roll(tensor, HD - ROT // 2, 1),
            jnp.where(lane < ROT, pltpu.roll(tensor, ROT // 2, 1), 0.0),
        )

    def turns_of(rows):
        table = turn_ref[rows, :]
        cos_rows = jnp.where(lane < ROT, table, 1.0)
        sin_rows = pltpu.roll(table, HD - ROT, 1)
        return cos_rows, sin_rows, table[:, 2 * ROT : 2 * ROT + 1]

    def project_piece(h, slot):
        rows = pl.ds(pl.multiple_of(slot * T, 128), T)
        cos_rows, sin_rows, _ = turns_of(rows)
        projected = nn(H1[rows, :], W[h, :, : 3 * HD]) + bias_h[h]
        first = projected[:, :HD]
        queries = (first * cos_rows + partner(first) * sin_rows).astype(jnp.bfloat16)
        second = projected[:, HD : 2 * HD]
        keys = (second * cos_rows + partner(second) * sin_rows).astype(jnp.bfloat16)
        values = projected[:, 2 * HD :].astype(jnp.bfloat16)
        start = pl.multiple_of(slot * T, 128)
        TA[h, :, pl.ds(start, HD)] = queries
        TA[h, :, pl.ds(start + HD, HD)] = keys
        TA[h, :, pl.ds(start + 2 * HD, HD)] = values

    def head_piece(h, slot):
        start = pl.multiple_of(slot * T, 128)
        rows = pl.ds(start, T)
        cos_rows, sin_rows, starts = turns_of(rows)
        queries = TA[h, :, pl.ds(start, HD)]
        keys = TA[h, :, pl.ds(start + HD, HD)]
        values = TA[h, :, pl.ds(start + 2 * HD, HD)]
        back = nn(DY[rows, :], W[h, :, 3 * HD :]).astype(jnp.bfloat16)
        contexts, grad_q = [], []
        grad_k, grad_v = [None, None], [None, None]
        for i in range(2):
            seen = QT * (i + 1)
            part = slice(QT * i, QT * (i + 1))
            raw = nt(queries[part], keys[:seen]) * scale
            query_at = lax.broadcasted_iota(jnp.int32, (QT, seen), 0) + QT * i
            key_at = lax.broadcasted_iota(jnp.int32, (QT, seen), 1)
            allowed = (key_at <= query_at) & (key_at.astype(jnp.float32) >= starts[part])
            scores = jnp.where(allowed, raw, -1e30)
            exponent = jnp.exp(scores - jnp.max(scores, axis=-1, keepdims=True))
            probs = exponent * (1.0 / jnp.sum(exponent, axis=-1, keepdims=True))
            soft = probs.astype(jnp.bfloat16)
            contexts.append(nn(soft, values[:seen]).astype(jnp.bfloat16))
            grad_probs = nt(back[part], values[:seen])
            inner = jnp.sum(probs * grad_probs, axis=-1, keepdims=True)
            grad_scores = (probs * (grad_probs - inner)).astype(jnp.bfloat16)
            grad_q.append((nn(grad_scores, keys[:seen]) * scale).astype(jnp.bfloat16))
            for j in range(i + 1):
                cut = slice(QT * j, QT * (j + 1))
                term_v = tn(soft[:, cut], back[part])
                term_k = tn(grad_scores[:, cut], queries[part])
                grad_v[j] = term_v if grad_v[j] is None else grad_v[j] + term_v
                grad_k[j] = term_k if grad_k[j] is None else grad_k[j] + term_k
        context = jnp.concatenate(contexts, axis=0)
        dq = jnp.concatenate(grad_q, axis=0).astype(jnp.float32)
        dk = (jnp.concatenate(grad_k, axis=0) * scale).astype(jnp.bfloat16).astype(jnp.float32)
        dv = jnp.concatenate(grad_v, axis=0)
        turned = jnp.concatenate(
            [
                dq * cos_rows - partner(dq) * sin_rows,
                dk * cos_rows - partner(dk) * sin_rows,
                dv,
            ],
            axis=1,
        ).astype(jnp.bfloat16)
        TA[h, : 3 * HD, rows] = turned.T
        TA[h, 3 * HD :, rows] = context.T
        total = jnp.sum(turned.astype(jnp.float32), axis=0, keepdims=True)
        qb[h] = jnp.where(slot == 0, total, qb[h] + total)

    def cut_piece(f, slot):
        rows = pl.ds(pl.multiple_of(slot * T, 128), T)
        k = HEADS_DEV + f
        pre = nn(H2[rows, :], W[k, :, :CUT]) + bias_f[f]
        grad = nn(DY[rows, :], W[k, :, CUT:])
        normal = 0.5 * (1.0 + lax.erf(pre * (0.5**0.5)))
        slope = normal + pre * (jnp.exp(-0.5 * pre * pre) * (0.5 * 0.7978845608028654))
        active = (pre * normal).astype(jnp.bfloat16)
        pulled = (grad * slope).astype(jnp.bfloat16)
        low = pl.multiple_of(f * WIDE, WIDE)
        H1[pl.ds(low, CUT), rows] = pulled.T
        H1[pl.ds(low + CUT, CUT), rows] = active.T
        total = jnp.sum(pulled.astype(jnp.float32), axis=0, keepdims=True)
        fb[f] = jnp.where(slot == 0, total, fb[f] + total)

    def grads(k, turned, left, edge):
        def step(j, carry):
            cols = pl.ds(pl.multiple_of(j * block, 128), block)
            G[lax.rem(k, 2), j, :edge, :] = nn(turned(0, edge), left[:, cols])
            G[lax.rem(k, 2), j, edge:, :] = nn(turned(edge, WIDE - edge), DY[:, cols])
            return carry

        lax.fori_loop(0, outer, step, 0)

    def head_turned(h):
        return lambda low, size: TA[h, pl.ds(low, size), :]

    def cut_turned(f):
        return lambda low, size: H1[pl.ds(pl.multiple_of(f * WIDE + low, 128), size), :]

    def rs_copy(k, way, t):
        to = b + INNER if way == 0 else b - INNER
        return remote(
            sbuf.at[way],
            rsb.at[way, t - 1],
            rs_s.at[k, way, t - 1],
            rs_r.at[k, way, t - 1],
            to,
            c,
        )

    def rs_sends(way, t):
        if way == 0:
            return (o <= t - 1) & (o <= outer - 2)
        return (o >= outer - t) & (o >= 1)

    def rs_receives(way, t):
        if way == 0:
            return (o >= 1) & (o <= t)
        return (o <= outer - 2) & (o >= outer - 1 - t)

    def rs_fetch(k, way, t):
        rs_copy(k, way, t).wait_recv()
        return rsb[way, t - 1].astype(jnp.float32)

    def rs_range(low, high):
        def step(n, carry):
            k = n // S
            t = lax.rem(n, S) + 1

            @pl.when((t == 1) & (k >= 1) & (o < outer - 1))
            def _():
                pl.semaphore_wait(free_s.at[0], 1)

            @pl.when((t == 1) & (k >= 1) & (o > 0))
            def _():
                pl.semaphore_wait(free_s.at[1], 1)

            for way in range(2):
                owner = o + outer - t if way == 0 else o - outer + t

                before = jnp.maximum(n - 1, 0)
                k_before = before // S
                t_before = lax.rem(before, S) + 1

                @pl.when((n >= 1) & rs_sends(way, t_before))
                def _():
                    rs_copy(k_before, way, t_before).wait_send()

                @pl.when(rs_sends(way, t))
                def _():
                    @pl.when(rs_receives(way, t - 1) & (t > 1))
                    def _():
                        sbuf[way] = (
                            G[lax.rem(k, 2), owner] + rs_fetch(k, way, t - 1)
                        ).astype(jnp.bfloat16)

                    @pl.when(jnp.logical_not(rs_receives(way, t - 1) & (t > 1)))
                    def _():
                        sbuf[way] = G[lax.rem(k, 2), owner].astype(jnp.bfloat16)

                    rs_copy(k, way, t).start()

            return carry

        lax.fori_loop(low, high, step, 0)

    def rs(low, high):
        rs_range(low * S // 3, high * S // 3)

    def gr_copy(k, d, received=False):
        to = near[d - 1]
        slot = lax.rem(to, INNER)
        return remote(
            fbuf.at[pl.ds(pl.multiple_of(slot * R, 16), R)],
            gr.at[k, slot if received else q],
            gr_s.at[k, d - 1],
            gr_r.at[k, d - 1],
            to,
            c,
        )

    def gr_local(k):
        return pltpu.make_async_copy(
            fbuf.at[pl.ds(pl.multiple_of(q * R, 16), R)],
            gr.at[k, q],
            gr_s.at[k, 3],
        )

    def gr_sent(k):
        for d in range(1, INNER):
            gr_copy(k, d).wait_send()
        gr_local(k).wait()

    def rs_final(k):
        for way in range(2):

            @pl.when(rs_receives(way, S))
            def _():
                G[lax.rem(k, 2), o] = G[lax.rem(k, 2), o] + rs_fetch(k, way, S)

        @pl.when((k < CHUNKS - 1) & (o > 0))
        def _():
            pl.semaphore_signal(
                free_s.at[0], inc=1, device_id=(b - INNER, c), device_id_type=MESH
            )

        @pl.when((k < CHUNKS - 1) & (o < outer - 1))
        def _():
            pl.semaphore_signal(
                free_s.at[1], inc=1, device_id=(b + INNER, c), device_id_type=MESH
            )

        @pl.when(k >= 1)
        def _():
            gr_sent(k - 1)

        final = G[lax.rem(k, 2), o].T
        cs[k] = jnp.sum(squares(final), axis=0, keepdims=True)
        fbuf[...] = final.astype(jnp.bfloat16)
        for d in range(1, INNER):
            gr_copy(k, d).start()
        gr_local(k).start()

    TILE = T // 2
    TILES = 2 * INNER
    PER_ROW = D // TILE

    def tile_slot(i):
        return INNER - 1 - i // 2

    def product(which, i, side):
        at = pl.multiple_of(tile_slot(i) * T + lax.rem(i, 2) * TILE, 128)
        toks = pl.ds(at, TILE)
        features = pl.ds(pl.multiple_of(side * half, 128), half)
        terms = []
        if which == 0:
            for h in range(HEADS_DEV):
                terms.append((h, slice(0, 3 * HD), lambda h=h: TA[h, : 3 * HD, toks]))
        elif which == 1:
            for f in range(CUTS):
                low = f * WIDE
                terms.append(
                    (HEADS_DEV + f, slice(0, CUT), lambda low=low: H1[low : low + CUT, toks])
                )
        else:
            for h in range(HEADS_DEV):
                terms.append((h, slice(3 * HD, WIDE), lambda h=h: TA[h, 3 * HD :, toks]))
            for f in range(CUTS):
                low = f * WIDE + CUT
                terms.append(
                    (HEADS_DEV + f, slice(CUT, WIDE), lambda low=low: H1[low : low + CUT, toks])
                )
        for place, (k, cols, right) in enumerate(terms):
            term = nn(W[k, features, cols], right())
            own[...] = term if place == 0 else own[...] + term

    def sib_copy(which, i):
        return remote(
            sib_send.at[lax.rem(i, 2)],
            sib_land.at[lax.rem(i, 4)],
            sib_s.at[which, i],
            sib_r.at[which, i],
            b,
            1 - c,
        )

    def plane_copy(which, i):
        slot = tile_slot(i)
        low, high = lax.rem(slot, 2), slot // 2
        to = b + low * (1 - 2 * lax.rem(b, 2)) + high * 2 * (1 - 2 * lax.rem(b // 2, 2))
        if which == 0:
            src = psend.at[lax.rem(i, 2)]
        else:
            t = (which - 1) * (TILES - 2) + i
            src = H2.at[
                pl.ds(pl.multiple_of(t // PER_ROW * half, 128), half),
                pl.ds(pl.multiple_of(lax.rem(t, PER_ROW) * TILE, 128), TILE),
            ]
        return remote(
            src,
            xr.at[which, slot - 1, lax.rem(i, 2)],
            p_s.at[which, i],
            p_r.at[which, i],
            to,
            c,
        )

    def tile_a(which, i):
        @pl.when(i >= 2)
        def _():
            sib_copy(which, i - 2).wait_send()

        product(which, i, 1 - c)
        sib_send[lax.rem(i, 2)] = own[...].astype(jnp.bfloat16)
        sib_copy(which, i).start()

    def tile_b(which, i):
        product(which, i, c)
        sib_copy(which, i).wait_recv()

        @pl.when(i < TILES - 2)
        def _():
            total = (own[...] + sib_land[lax.rem(i, 4)].astype(jnp.float32)).astype(jnp.bfloat16)
            if which == 0:

                @pl.when(i >= 2)
                def _():
                    plane_copy(which, i - 2).wait_send()

                psend[lax.rem(i, 2)] = total
            else:
                t = (which - 1) * (TILES - 2) + i
                H2[
                    pl.ds(pl.multiple_of(t // PER_ROW * half, 128), half),
                    pl.ds(pl.multiple_of(lax.rem(t, PER_ROW) * TILE, 128), TILE),
                ] = total
            plane_copy(which, i).start()

        @pl.when(i >= TILES - 2)
        def _():
            own[...] = own[...] + sib_land[lax.rem(i, 4)].astype(jnp.float32)
            keep = pltpu.make_async_copy(own, xo.at[which, lax.rem(i, 2)], tmp_s.at[2])
            keep.start()
            keep.wait()

    def sum_tiles(which, beside):
        tile_a(which, 0)

        def step(i, carry):
            @pl.when(i < TILES - 1)
            def _():
                tile_a(which, i + 1)

            tile_b(which, i)
            beside(i)
            return carry

        lax.fori_loop(0, TILES, step, 0)

    def sum_sent(which):
        for i in range(TILES - 2, TILES):
            sib_copy(which, i).wait_send()
        for i in range(TILES - 4, TILES - 2):
            plane_copy(which, i).wait_send()

    def share(low, high, i, pieces, run):
        first, last = low * S // 3, high * S // 3
        steps = last - first
        run(
            first + (steps * i + pieces - 1) // pieces,
            first + (steps * (i + 1) + pieces - 1) // pieces,
        )

    a2a_start(0)
    gather_one(0, xin, H1)
    a2a_start(1)
    ag(0, 1)
    gather_two(0, xin, H1)
    gather_one(1, yin, DY)
    a2a_start(2)
    ag(1, 2)
    x_local(0, xin, H1).wait()
    sx_wait(0, H1, 0)
    norm_rows(0)
    ag(2, 3)
    gather_three(0, xin, H1)
    gather_two(1, yin, DY)
    for k in range(3, CHUNKS):
        a2a_start(k)
    gather_sent(0, xin, H1)
    for slot in range(1, INNER):
        sx_wait(0, H1, slot)
        norm_rows(slot)
        ag(2 + slot, 3 + slot)

    def project_step(h, carry):
        ag_wait(h, S)

        def slot_step(slot, inner_carry):
            project_piece(h, slot)
            return inner_carry

        lax.fori_loop(0, INNER, slot_step, 0)
        ag(6 + h, 7 + h)
        return carry

    project_step(0, 0)
    gather_three(1, yin, DY)
    project_step(1, 0)
    x_local(1, yin, DY).wait()
    for slot in range(INNER):
        sx_wait(1, DY, slot)
    gather_sent(1, yin, DY)

    def head_step(h, carry):
        def slot_step(slot, inner_carry):
            head_piece(h, slot)
            share(8 + 2 * h, 10 + 2 * h, slot, INNER, ag_range)
            share(0, 3 * h, slot, INNER, rs_range)
            return inner_carry

        lax.fori_loop(0, INNER, slot_step, 0)
        grads(h, head_turned(h), H1, 3 * HD)

        @pl.when(h == 1)
        def _():
            rs_final(0)

        return carry

    lax.fori_loop(0, HEADS_DEV, head_step, 0)

    def beside_one(i):
        share(12, 13, i, TILES, ag_range)
        share(3, 6, i, TILES, rs_range)

    sum_tiles(0, beside_one)

    def cut_step(f, carry):
        ag_wait(HEADS_DEV + f, S)

        def slot_step(slot, inner_carry):
            cut_piece(f, slot)
            share(
                jnp.minimum(13 + 2 * f, 18), jnp.minimum(15 + 2 * f, 18), slot, INNER, ag_range
            )
            share(jnp.maximum(6, 3 + 3 * f), 6 + 3 * f, slot, INNER, rs_range)
            return inner_carry

        lax.fori_loop(0, INNER, slot_step, 0)
        grads(HEADS_DEV + f, cut_turned(f), H2, CUT)
        rs_final(1 + f)
        return carry

    lax.fori_loop(0, CUTS, cut_step, 0)
    sum_sent(0)
    sum_tiles(1, lambda i: share(15, 18, i, TILES, rs_range))
    for i in range(TILES - 2, TILES):
        sib_copy(1, i).wait_send()

    def beside_last(i):
        @pl.when(i == 1)
        def _():
            rs_final(CHUNKS - 1)

    sum_tiles(2, beside_last)
    for i in range(TILES - 2, TILES):
        sib_copy(2, i).wait_send()

    gr_sent(CHUNKS - 1)

    def drain_chunk(k, carry):
        for d in range(1, INNER):
            a2a_copy(k, d).wait_send()
            gr_copy(k, d, True).wait_recv()

        def drain_step(s, inner_carry):
            ag_sends(k, s, lambda copy: copy.wait_send())
            return inner_carry

        lax.fori_loop(1, S + 1, drain_step, 0)
        return carry

    lax.fori_loop(0, CHUNKS, drain_chunk, 0)
    for way in range(2):

        @pl.when(rs_sends(way, S))
        def _():
            rs_copy(CHUNKS - 1, way, S).wait_send()

    for which in range(3):

        def drain_tile(i, carry):
            if which:
                plane_copy(which, i).wait_send()
            plane_copy(which, i).wait_recv()
            return carry

        lax.fori_loop(0, TILES - 2, drain_tile, 0)


def block_call(count, wst, xin, yin, turns, norm_params, bias_h, bias_f):
    outer = count // INNER
    S = outer - 1
    tokens, half = xin.shape
    group = INNER * tokens
    rows = wst.shape[2]
    tile = tokens // 2
    low, high = jnp.bfloat16, jnp.float32
    any_spec = pl.BlockSpec(memory_space=pl.ANY)
    vmem_spec = pl.BlockSpec(memory_space=pltpu.VMEM)
    dma = pltpu.SemaphoreType.DMA
    return pl.pallas_call(
        functools.partial(block_kernel, count),
        out_shape=[
            jax.ShapeDtypeStruct((CHUNKS, INNER, rows, WIDE), low),
            jax.ShapeDtypeStruct((3, INNER - 1, 2, half, tile), low),
            jax.ShapeDtypeStruct((3, 2, half, tile), high),
            jax.ShapeDtypeStruct((HEADS_DEV, 1, 3 * HD), high),
            jax.ShapeDtypeStruct((CUTS, 1, CUT), high),
            jax.ShapeDtypeStruct((CHUNKS, 1, WIDE), high),
            jax.ShapeDtypeStruct((tokens, 128), high),
        ],
        in_specs=[any_spec] * 3 + [vmem_spec] * 4,
        out_specs=[any_spec] * 3 + [vmem_spec] * 4,
        scratch_shapes=[
            pltpu.VMEM((group, D), low),
            pltpu.VMEM((group, D), low),
            pltpu.VMEM((group, D), low),
            pltpu.VMEM((CHUNKS, D, WIDE), low),
            pltpu.VMEM((HEADS_DEV, WIDE, group), low),
            pltpu.VMEM((2, outer, WIDE, INNER * rows), high),
            pltpu.VMEM((2, WIDE, INNER * rows), low),
            pltpu.VMEM((INNER * rows, WIDE), low),
            pltpu.VMEM((2, S, WIDE, INNER * rows), low),
            pltpu.VMEM((2, half, tile), low),
            pltpu.VMEM((4, half, tile), low),
            pltpu.VMEM((2, half, tile), low),
            pltpu.VMEM((half, tile), high),
            dma((CHUNKS, INNER - 1)),
            dma((CHUNKS, INNER - 1)),
            dma((CHUNKS,)),
            dma((CHUNKS, 2, S)),
            dma((CHUNKS, 2, S)),
            dma((2, INNER - 1)),
            dma((2, INNER - 1)),
            dma((2, INNER)),
            dma((2, INNER)),
            dma((CHUNKS, 2, S)),
            dma((CHUNKS, 2, S)),
            dma((CHUNKS, INNER)),
            dma((CHUNKS, INNER - 1)),
            dma((3, 2 * INNER)),
            dma((3, 2 * INNER)),
            dma((3, 2 * INNER)),
            dma((3, 2 * INNER)),
            dma((3,)),
            pltpu.SemaphoreType.REGULAR((2,)),
        ],
        compiler_params=pltpu.CompilerParams(
            collective_id=0, has_side_effects=True, vmem_limit_bytes=64 * 1024 * 1024
        ),
        cost_estimate=pl.CostEstimate(
            flops=80_000_000_000, bytes_accessed=60_000_000, transcendentals=10_000_000
        ),
    )(wst, xin, yin, turns, norm_params, bias_h, bias_f)


SLOT_ROWS = 16


def total_of(values):
    return jnp.sum(jnp.sum(values, axis=0, keepdims=True), axis=1, keepdims=True)


def tail_kernel(
    count,
    gr,
    wq,
    wo,
    w1,
    w2,
    xr,
    xo,
    xin,
    yin,
    st,
    norm_ref,
    pb,
    fcb,
    row_old,
    qc_old,
    or_old,
    f1_old,
    f2_old,
    norm_second,
    bias_second,
    fcb_second,
    cs,
    qb,
    fb,
    out_ref,
    ing_ref,
    row_new,
    qc_new,
    or_new,
    f1_new,
    f2_new,
    norm_grad,
    norm_moment,
    norm_new,
    bias_grad,
    bias_moment,
    bias_new,
    fcb_grad,
    fcb_moment,
    fcb_new,
    coef,
    scaled_buf,
    normed_buf,
    terms,
    terms_in,
    rsum,
    rsum_in,
    pay,
    z_in,
    z_sum,
    p_in,
    p_sum,
    s_in,
    pay2,
    z2_in,
    z2_sum,
    p2_in,
    p2_sum,
    s2_in,
    z_s,
    z_r,
    p_s,
    p_r,
    s_s,
    s_r,
):
    outer = count // INNER
    T, half = xin.shape
    R = gr.shape[2]
    b = lax.axis_index("batch")
    c = lax.axis_index("branch")
    q = lax.rem(b, INNER)
    o = b // INNER
    bx, by = flip(b, 1), flip(b, 2)
    near = (bx, by, flip(bx, 2))
    on_b = (b == 0).astype(jnp.float32)
    on_c = (c == 0).astype(jnp.float32)

    def remote(src, dst, ssem, rsem, to_b, to_c):
        return pltpu.make_async_remote_copy(
            src_ref=src,
            dst_ref=dst,
            send_sem=ssem,
            recv_sem=rsem,
            device_id=(to_b, to_c),
            device_id_type=MESH,
        )

    def chain(d):
        return lax.rem(o + d, outer)

    barrier = pltpu.get_barrier_semaphore()
    for who in near:
        pl.semaphore_signal(barrier, inc=1, device_id=(who, c), device_id_type=MESH)
    pl.semaphore_signal(barrier, inc=1, device_id=(b, 1 - c), device_id_type=MESH)
    for d in range(1, outer):
        pl.semaphore_signal(
            barrier, inc=1, device_id=(chain(d) * INNER + q, c), device_id_type=MESH
        )

    HALF_T = T // 2
    lane_t = lax.broadcasted_iota(jnp.int32, (HALF_T, 128), 1)
    own_half = pl.ds(pl.multiple_of(c * half, 128), half)
    other_half = pl.ds(pl.multiple_of((1 - c) * half, 128), half)
    gain_a = norm_ref[0:1, own_half]
    gain_b = norm_ref[2:3, own_half]
    pay[...] = jnp.zeros_like(pay)
    for i in range(2):
        rows = slice(i * HALF_T, (i + 1) * HALF_T)

        def whole(which):
            return (
                xo[which, i]
                + xr[which, 0, i].astype(jnp.float32)
                + xr[which, 1, i].astype(jnp.float32)
                + xr[which, 2, i].astype(jnp.float32)
            ).T

        values = xin[rows, :].astype(jnp.float32)
        out_ref[rows, :] = (values + whole(2) + pb[3:4, :] + pb[4:5, :]).astype(jnp.bfloat16)
        normed = (values - st[rows, 0:1]) * st[rows, 1:2]
        one = whole(0)
        two = whole(1)
        scaled = one * gain_a + two * gain_b
        scaled_buf[rows, :] = scaled
        normed_buf[rows, :] = normed
        terms[rows, :] = jnp.where(
            lane_t == 0,
            jnp.sum(scaled, axis=1, keepdims=True),
            jnp.where(lane_t == 1, jnp.sum(scaled * normed, axis=1, keepdims=True), 0.0),
        )
        pay[5:6, :] += jnp.sum(one * normed, axis=0, keepdims=True)
        pay[6:7, :] += jnp.sum(one, axis=0, keepdims=True)
        pay[7:8, :] += jnp.sum(two * normed, axis=0, keepdims=True)
        pay[8:9, :] += jnp.sum(two, axis=0, keepdims=True)
        pay[9:10, :] += jnp.sum(yin[rows, :].astype(jnp.float32), axis=0, keepdims=True)
    for k in range(CHUNKS):
        pay[k // 2 : k // 2 + 1, k % 2 * WIDE : (k % 2 + 1) * WIDE] = cs[k]
    for h in range(HEADS_DEV):
        pay[3:4, h * 3 * HD : (h + 1) * 3 * HD] = qb[h]
    for f in range(CUTS):
        pay[4:5, f * CUT : (f + 1) * CUT] = fb[f]
    lane_p = lax.broadcasted_iota(jnp.int32, (1, half), 1)
    biases = jnp.sum(pb[...] * pb[...], axis=1, keepdims=True) * on_b
    scalars = (
        [total_of(w[...] * w[...]) for w in (wq, wo, w1, w2)]
        + [biases[i : i + 1] for i in range(5)]
        + [total_of(fcb[...] * fcb[...]) * on_b]
    )
    line = jnp.zeros((1, half), jnp.float32)
    for place, value in enumerate(scalars):
        line = jnp.where(lane_p == place, value, line)
    pay[10:11, :] = line

    pl.semaphore_wait(barrier, INNER + outer - 1)

    def chain_sends(src, buf, base, what):
        for d in range(1, outer):
            what(
                remote(
                    src,
                    buf.at[o],
                    z_s.at[base, d - 1],
                    z_r.at[base, d - 1],
                    chain(d) * INNER + q,
                    c,
                )
            )

    def chain_waits(src, buf, base):
        for d in range(1, outer):
            source = chain(outer - d)
            remote(
                src,
                buf.at[source],
                z_s.at[base, d - 1],
                z_r.at[base, d - 1],
                source * INNER + q,
                c,
            ).wait_recv()

    def plane_sends(src, buf, base, what):
        for d in range(1, INNER):
            what(remote(src, buf.at[q], p_s.at[base, d - 1], p_r.at[base, d - 1], near[d - 1], c))

    def plane_waits(src, buf, base):
        for d in range(1, INNER):
            remote(
                src,
                buf.at[lax.rem(near[d - 1], INNER)],
                p_s.at[base, d - 1],
                p_r.at[base, d - 1],
                near[d - 1],
                c,
            ).wait_recv()

    def pair_copy(src, dst, place):
        return remote(src, dst, s_s.at[place], s_r.at[place], b, 1 - c)

    start = lambda copy: copy.start()
    chain_sends(pay, z_in, 0, start)
    z_in[o] = pay[...]
    pair_copy(terms, terms_in, 0).start()

    lane_r = lax.broadcasted_iota(jnp.int32, (R, 128), 1)
    head_square = jnp.zeros((R, WIDE), jnp.float32)
    cut_square = jnp.zeros((R, WIDE), jnp.float32)
    for part in range(INNER):
        for k in range(CHUNKS):
            gradient = gr[k, part].astype(jnp.float32)
            if k < HEADS_DEV:
                head_square = head_square + squares(gradient)
            else:
                cut_square = cut_square + squares(gradient)
    pieces = (
        jnp.sum(head_square[:, : 3 * HD], axis=1, keepdims=True),
        jnp.sum(cut_square[:, :CUT], axis=1, keepdims=True),
        jnp.sum(head_square[:, 3 * HD :], axis=1, keepdims=True),
        jnp.sum(cut_square[:, CUT:], axis=1, keepdims=True),
    )
    line = jnp.zeros((R, 128), jnp.float32)
    for place, value in enumerate(pieces):
        line = jnp.where(lane_r == place, value, line)
    rsum[...] = line
    pair_copy(rsum, rsum_in, 1).start()

    pair_copy(terms, terms_in, 0).wait_recv()
    for i in range(2):
        rows = slice(i * HALF_T, (i + 1) * HALF_T)
        both = terms[rows, :] + terms_in[rows, :]
        ing_ref[rows, :] = (
            st[rows, 1:2]
            * (
                scaled_buf[rows, :]
                - both[:, 0:1] / D
                - normed_buf[rows, :] * (both[:, 1:2] / D)
            )
            + yin[rows, :].astype(jnp.float32)
        ).astype(jnp.bfloat16)
    pair_copy(rsum, rsum_in, 1).wait_recv()
    rows_after = renew_stat(row_old[...], (rsum[...] + rsum_in[...])[:, :4])
    row_new[...] = rows_after

    chain_waits(pay, z_in, 0)
    acc = z_in[0]
    for j in range(1, outer):
        acc = acc + z_in[j]
    z_sum[...] = acc
    plane_sends(z_sum, p_in, 0, start)
    p_in[q] = acc
    plane_waits(z_sum, p_in, 0)
    p_sum[...] = p_in[0] + p_in[1] + p_in[2] + p_in[3]
    pair_copy(p_sum, s_in, 2).start()

    inverse_rows = 1.0 / rows_after
    head_acc = [jnp.zeros((R, 3 * HD), jnp.float32), jnp.zeros((R, HD), jnp.float32)]
    cut_acc = [jnp.zeros((R, CUT), jnp.float32), jnp.zeros((R, CUT), jnp.float32)]
    for part in range(INNER):
        sums = p_in[part]
        for h in range(HEADS_DEV):
            gradient = gr[h, part].astype(jnp.float32)
            square = gradient * gradient
            found = sums[h // 2 : h // 2 + 1, h % 2 * WIDE : (h % 2 + 1) * WIDE]
            cols = pl.ds(part * HEADS_DEV * HD + h * HD, HD)
            parts = []
            for p in range(3):
                fresh = renew_stat(qc_old[p : p + 1, cols], found[:, p * HD : (p + 1) * HD])
                qc_new[p : p + 1, cols] = fresh
                parts.append(1.0 / fresh)
            head_acc[0] = head_acc[0] + square[:, : 3 * HD] * jnp.concatenate(parts, axis=1)
            fresh = renew_stat(or_old[:, cols], found[:, 3 * HD :])
            or_new[:, cols] = fresh
            head_acc[1] = head_acc[1] + square[:, 3 * HD :] * (1.0 / fresh)
        for f in range(CUTS):
            k = HEADS_DEV + f
            gradient = gr[k, part].astype(jnp.float32)
            square = gradient * gradient
            found = sums[k // 2 : k // 2 + 1, k % 2 * WIDE : (k % 2 + 1) * WIDE]
            cols = slice(f * CUT, (f + 1) * CUT)
            fresh = renew_stat(f1_old[part : part + 1, cols], found[:, :CUT])
            f1_new[part, :, cols] = fresh
            cut_acc[0] = cut_acc[0] + square[:, :CUT] * (1.0 / fresh)
            fresh = renew_stat(f2_old[part : part + 1, cols], found[:, CUT:])
            f2_new[part, :, cols] = fresh
            cut_acc[1] = cut_acc[1] + square[:, CUT:] * (1.0 / fresh)
    for part in range(INNER):
        for h in range(HEADS_DEV):
            for p in range(3):
                low = h * 3 * HD + p * HD
                bias_grad[p : p + 1, pl.ds(part * HEADS_DEV * HD + h * HD, HD)] = p_in[
                    part, 3:4, low : low + HD
                ]
        fcb_grad[part : part + 1, :] = p_in[part, 4:5, :]
    bias_grad[3:4, :] = p_sum[9:10, :]
    bias_grad[4:5, :] = p_sum[9:10, :]
    bias_after, bias_update = second_step(bias_grad[...], bias_second[...])
    bias_moment[...] = bias_after
    fcb_after, fcb_update = second_step(fcb_grad[...], fcb_second[...])
    fcb_moment[...] = fcb_after
    usq = jnp.sum(bias_update * bias_update, axis=1, keepdims=True) * on_b
    scalars = (
        [
            total_of(rows_after[:, 0:1]) * on_c,
            total_of(head_acc[0] * inverse_rows[:, 0:1]),
            total_of(rows_after[:, 1:2]) * on_c,
            total_of(cut_acc[0] * inverse_rows[:, 1:2]),
            total_of(or_new[...]) * on_b,
            total_of(head_acc[1] * inverse_rows[:, 2:3]),
            sum(total_of(f2_new[part]) for part in range(INNER)) * on_b,
            total_of(cut_acc[1] * inverse_rows[:, 3:4]),
        ]
        + [usq[i : i + 1] for i in range(5)]
        + [total_of(fcb_update * fcb_update) * on_b]
    )
    lane_s = lax.broadcasted_iota(jnp.int32, (8, 128), 1)
    line = jnp.zeros((8, 128), jnp.float32)
    for place, value in enumerate(scalars):
        line = jnp.where(lane_s == place, value, line)
    pay2[...] = line
    chain_sends(pay2, z2_in, 1, start)
    z2_in[o] = line

    pair_copy(p_sum, s_in, 2).wait_recv()
    norm_grad[:, own_half] = p_sum[5:9, :]
    norm_grad[:, other_half] = s_in[5:9, :]
    old = p_sum[10:11, :] + s_in[10:11, :]
    norm_after, norm_update = second_step(norm_grad[...], norm_second[...])
    norm_moment[...] = norm_after

    def moved(vector, update, update_square, old_square, entries):
        clip_factor = jnp.maximum(1.0, jnp.sqrt(update_square / entries))
        step_rate = RATE * jnp.maximum(FLOOR_RATE, jnp.sqrt(old_square / entries))
        return vector - step_rate * update / clip_factor

    norm_values = norm_ref[...]
    norm_new[...] = moved(
        norm_values,
        norm_update,
        jnp.sum(norm_update * norm_update, axis=1, keepdims=True),
        jnp.sum(norm_values * norm_values, axis=1, keepdims=True),
        D,
    )

    chain_waits(pay2, z2_in, 1)
    acc = z2_in[0]
    for j in range(1, outer):
        acc = acc + z2_in[j]
    z2_sum[...] = acc
    plane_sends(z2_sum, p2_in, 1, start)
    p2_in[q] = acc
    plane_waits(z2_sum, p2_in, 1)
    acc = p2_in[0] + p2_in[1] + p2_in[2] + p2_in[3]
    p2_sum[...] = acc
    pair_copy(p2_sum, s2_in, 3).start()
    pair_copy(p2_sum, s2_in, 3).wait_recv()
    sums = (acc + s2_in[...])[0:1, :]

    def scalar(place):
        return sums[:, place : place + 1]

    def factor(total, inverse, place, entries):
        clip_factor = jnp.maximum(1.0, jnp.sqrt(total * inverse / entries))
        rate = RATE * jnp.maximum(FLOOR_RATE, jnp.sqrt(old[:, place : place + 1] / entries))
        return rate * jnp.sqrt(total) / clip_factor

    factors = (
        factor(scalar(0), scalar(1), 0, 3 * D * D),
        factor(scalar(2), scalar(3), 2, D * FF),
        factor(scalar(4), scalar(5), 1, D * D),
        factor(scalar(6), scalar(7), 3, FF * D),
    )
    line = jnp.zeros((8, 128), jnp.float32)
    for place, value in enumerate(factors):
        line = jnp.where(lane_s == place, value, line)
    coef[...] = line
    for i in range(5):
        bias_new[i : i + 1, :] = moved(
            pb[i : i + 1, :], bias_update[i : i + 1], scalar(8 + i), old[:, 4 + i : 5 + i], D
        )
    fcb_new[...] = moved(fcb[...], fcb_update, scalar(13), old[:, 9:10], FF)

    finish = lambda copy: copy.wait_send()
    chain_sends(pay, z_in, 0, finish)
    chain_sends(pay2, z2_in, 1, finish)
    plane_sends(z_sum, p_in, 0, finish)
    plane_sends(z2_sum, p2_in, 1, finish)
    pair_copy(terms, terms_in, 0).wait_send()
    pair_copy(rsum, rsum_in, 1).wait_send()
    pair_copy(p_sum, s_in, 2).wait_send()
    pair_copy(p2_sum, s2_in, 3).wait_send()


def tail_call(count, *args):
    outer = count // INNER
    received, xin = args[0], args[7]
    tokens, half = xin.shape
    rows = received.shape[2]
    high = jnp.float32
    spec = pl.BlockSpec(memory_space=pltpu.VMEM)
    dma = pltpu.SemaphoreType.DMA

    def out(*shape, dtype=high):
        return jax.ShapeDtypeStruct(shape, dtype)

    outs = [
        out(tokens, half, dtype=jnp.bfloat16),
        out(tokens, half, dtype=jnp.bfloat16),
        out(rows, 4),
        out(3, half),
        out(1, half),
        out(INNER, 1, half),
        out(INNER, 1, half),
        out(4, D),
        out(4, D),
        out(4, D),
        out(5, half),
        out(5, half),
        out(5, half),
        out(INNER, half),
        out(INNER, half),
        out(INNER, half),
        out(8, 128),
    ]
    slot = (SLOT_ROWS, half)
    return pl.pallas_call(
        functools.partial(tail_kernel, count),
        out_shape=outs,
        in_specs=[spec] * len(args),
        out_specs=[spec] * len(outs),
        scratch_shapes=[
            pltpu.VMEM((tokens, half), high),
            pltpu.VMEM((tokens, half), high),
            pltpu.VMEM((tokens, 128), high),
            pltpu.VMEM((tokens, 128), high),
            pltpu.VMEM((rows, 128), high),
            pltpu.VMEM((rows, 128), high),
            pltpu.VMEM(slot, high),
            pltpu.VMEM((outer, *slot), high),
            pltpu.VMEM(slot, high),
            pltpu.VMEM((INNER, *slot), high),
            pltpu.VMEM(slot, high),
            pltpu.VMEM(slot, high),
            pltpu.VMEM((8, 128), high),
            pltpu.VMEM((outer, 8, 128), high),
            pltpu.VMEM((8, 128), high),
            pltpu.VMEM((INNER, 8, 128), high),
            pltpu.VMEM((8, 128), high),
            pltpu.VMEM((8, 128), high),
            dma((2, outer - 1)),
            dma((2, outer - 1)),
            dma((2, INNER - 1)),
            dma((2, INNER - 1)),
            dma((4,)),
            dma((4,)),
        ],
        compiler_params=pltpu.CompilerParams(
            collective_id=1, has_side_effects=True, vmem_limit_bytes=58 * 1024 * 1024
        ),
        cost_estimate=pl.CostEstimate(
            flops=50_000_000, bytes_accessed=40_000_000, transcendentals=100_000
        ),
    )(*args)


def update_kernel(
    gr,
    wq,
    wo,
    w1,
    w2,
    row_new,
    qc_new,
    or_new,
    f1_new,
    f2_new,
    coef,
    q_grad,
    q_next,
    q_copy,
    o_grad,
    o_next,
    o_copy,
    f1_grad,
    f1_next,
    f1_copy,
    f2_grad,
    f2_next,
    f2_copy,
):
    side = lax.rsqrt(row_new[...]) * coef[0:1, :4]

    def put(grad_ref, next_ref, copy_ref, where, weight, gradient, update):
        fresh = weight[where] - update
        grad_ref[where] = gradient
        next_ref[where] = fresh
        copy_ref[where] = fresh.astype(jnp.bfloat16)

    for h in range(HEADS_DEV):
        gradient = gr[h, 0].astype(jnp.float32)
        for p in range(3):
            mine = gradient[:, p * HD : (p + 1) * HD]
            update = mine * side[:, 0:1] * lax.rsqrt(qc_new[p : p + 1, h * HD : (h + 1) * HD])
            where = (p, slice(None), slice(h * HD, (h + 1) * HD))
            put(q_grad, q_next, q_copy, where, wq, mine, update)
        mine = gradient[:, 3 * HD :]
        update = mine * side[:, 2:3] * lax.rsqrt(or_new[:, h * HD : (h + 1) * HD])
        where = (slice(h * HD, (h + 1) * HD), slice(None))
        put(o_grad, o_next, o_copy, where, wo, mine.T, update.T)
    for f in range(CUTS):
        gradient = gr[HEADS_DEV + f, 0].astype(jnp.float32)
        cols = slice(f * CUT, (f + 1) * CUT)
        mine = gradient[:, :CUT]
        update = mine * side[:, 1:2] * lax.rsqrt(f1_new[0, :, cols])
        put(f1_grad, f1_next, f1_copy, (slice(None), cols), w1, mine, update)
        mine = gradient[:, CUT:]
        update = mine * side[:, 3:4] * lax.rsqrt(f2_new[0, :, cols])
        put(f2_grad, f2_next, f2_copy, (cols, slice(None)), w2, mine.T, update.T)


def update_call(gr, wq, wo, w1, w2, row_new, qc_new, or_new, f1_new, f2_new, coef):
    rows = gr.shape[2]
    width_q = HEADS_DEV * HD
    hidden_q = CUTS * CUT
    spec = pl.BlockSpec
    q_spec = spec((3, rows, width_q), lambda i: (0, 0, i))
    o_spec = spec((width_q, rows), lambda i: (i, 0))
    f1_spec = spec((rows, hidden_q), lambda i: (0, i))
    f2_spec = spec((hidden_q, rows), lambda i: (i, 0))
    outs, out_specs = [], []
    for array, its in ((wq, q_spec), (wo, o_spec), (w1, f1_spec), (w2, f2_spec)):
        for dtype in (jnp.float32, jnp.float32, jnp.bfloat16):
            outs.append(jax.ShapeDtypeStruct(array.shape, dtype))
            out_specs.append(its)
    return pl.pallas_call(
        update_kernel,
        grid=(INNER,),
        out_shape=outs,
        in_specs=[
            spec((CHUNKS, 1, rows, WIDE), lambda i: (0, i, 0, 0)),
            q_spec,
            o_spec,
            f1_spec,
            f2_spec,
            spec((rows, 4), lambda i: (0, 0)),
            spec((3, width_q), lambda i: (0, i)),
            spec((1, width_q), lambda i: (0, i)),
            spec((1, 1, hidden_q), lambda i: (i, 0, 0)),
            spec((1, 1, hidden_q), lambda i: (i, 0, 0)),
            spec((8, 128), lambda i: (0, 0)),
        ],
        out_specs=out_specs,
        compiler_params=pltpu.CompilerParams(vmem_limit_bytes=48 * 1024 * 1024),
        cost_estimate=pl.CostEstimate(
            flops=20_000_000, bytes_accessed=30_000_000, transcendentals=100_000
        ),
    )(gr, wq, wo, w1, w2, row_new, qc_new, or_new, f1_new, f2_new, coef)


def swap_pairs(count, step):
    return [(i, i ^ step) for i in range(count)]


def block_of(array, index, size, axis=0):
    return lax.dynamic_slice_in_dim(array, index * size, size, axis)


def on_device(
    inputs,
    cotangent,
    segment_ids,
    w_qkv,
    w_out,
    w_fc1,
    w_fc2,
    norm_params,
    proj_bias,
    fc1_bias,
    qkv_rows,
    qkv_cols,
    out_rows,
    out_cols,
    fc1_rows,
    fc1_cols,
    fc2_rows,
    fc2_cols,
    norm_second,
    bias_second,
    fc1b_second,
):
    tokens = inputs.shape[0]
    local_width = inputs.shape[1]
    local_hidden = fc1_bias.shape[0]
    rows = w_qkv.shape[0]
    count = lax.axis_size("batch")
    c = lax.axis_index("branch")
    b = lax.axis_index("batch")
    q = lax.rem(b, INNER)
    group = INNER * tokens
    width_q = local_width // INNER
    hidden_q = local_hidden // INNER
    qkv_low = w_qkv.astype(jnp.bfloat16).reshape(rows, 3, INNER, HEADS_DEV, HD)
    out_low = w_out.astype(jnp.bfloat16).reshape(INNER, HEADS_DEV, HD, rows)
    fc1_low = w_fc1.astype(jnp.bfloat16).reshape(rows, INNER, CUTS, CUT)
    fc2_low = w_fc2.astype(jnp.bfloat16).reshape(INNER, CUTS, CUT, rows)
    heads_low = jnp.concatenate(
        [
            qkv_low.transpose(3, 2, 0, 1, 4).reshape(HEADS_DEV, INNER, rows, 3 * HD),
            out_low.transpose(1, 0, 3, 2),
        ],
        axis=3,
    )
    cuts_low = jnp.concatenate(
        [fc1_low.transpose(2, 1, 0, 3), fc2_low.transpose(1, 0, 3, 2)], axis=3
    )
    wst = jnp.concatenate([heads_low, cuts_low], axis=0)

    segment = jnp.concatenate(
        [segment_ids]
        + [lax.ppermute(segment_ids, "batch", swap_pairs(count, d)) for d in range(1, INNER)],
        axis=0,
    )
    positions_idx = jnp.arange(tokens)
    earlier = jnp.sum((segment[:, None, :] < segment[:, :, None]).astype(jnp.int32), axis=2)
    starts = earlier.astype(jnp.float32).reshape(group, 1)
    places = (positions_idx[None] - earlier).astype(jnp.float32).reshape(group, 1)
    frequency = 10000.0 ** (-2.0 * jnp.arange(ROT // 2, dtype=jnp.float32) / ROT)
    angles = places * frequency[None, :]
    cos_part = jnp.cos(angles)
    sin_part = jnp.sin(angles)
    rest = (group, HD - 2 * ROT)
    turns = jnp.concatenate(
        [cos_part, cos_part, -sin_part, sin_part, jnp.broadcast_to(starts, rest)], axis=1
    )
    bias_h = (
        block_of(proj_bias[0:3], q, width_q, 1)
        .reshape(3, HEADS_DEV, HD)
        .transpose(1, 0, 2)
        .reshape(HEADS_DEV, 1, 3 * HD)
    )
    bias_f = block_of(fc1_bias, q, hidden_q).reshape(CUTS, 1, CUT)
    received, plane_parts, plane_own, head_bias, cut_bias, col_sums, row_moments = block_call(
        count, wst, inputs, cotangent, turns, norm_params, bias_h, bias_f
    )
    by_part = (INNER, hidden_q)
    qkv_parts = w_qkv.transpose(1, 0, 2)
    (
        output,
        input_grad,
        row_stats,
        qkv_cols_new,
        out_rows_new,
        fc1_cols_new,
        fc2_rows_new,
        norm_grad,
        norm_moment,
        norm_new,
        bias_grad,
        bias_moment,
        bias_new,
        fc1b_grad,
        fc1b_moment,
        fc1b_new,
        factors,
    ) = tail_call(
        count,
        received,
        qkv_parts.reshape(3 * rows, local_width),
        w_out,
        w_fc1,
        w_fc2,
        plane_parts,
        plane_own,
        inputs,
        cotangent,
        row_moments,
        norm_params,
        proj_bias,
        fc1_bias.reshape(by_part),
        jnp.stack([qkv_rows, fc1_rows, out_cols, fc2_cols], axis=1),
        qkv_cols,
        out_rows.reshape(1, local_width),
        fc1_cols.reshape(by_part),
        fc2_rows.reshape(by_part),
        norm_second,
        bias_second,
        fc1b_second.reshape(by_part),
        col_sums,
        head_bias,
        cut_bias,
    )
    updated = update_call(
        received,
        qkv_parts,
        w_out,
        w_fc1,
        w_fc2,
        row_stats,
        qkv_cols_new,
        out_rows_new,
        fc1_cols_new,
        fc2_rows_new,
        factors,
    )
    qkv_grad, qkv_next, qkv_copy = (array.transpose(1, 0, 2) for array in updated[0:3])
    out_grad, out_next, out_copy = updated[3:6]
    fc1_grad, fc1_next, fc1_copy = updated[6:9]
    fc2_grad, fc2_next, fc2_copy = updated[9:12]
    return (
        output,
        input_grad,
        qkv_grad,
        qkv_next,
        row_stats[:, 0],
        qkv_cols_new,
        qkv_copy,
        out_grad,
        out_next,
        out_rows_new.reshape(local_width),
        row_stats[:, 2],
        out_copy,
        fc1_grad,
        fc1_next,
        row_stats[:, 1],
        fc1_cols_new.reshape(local_hidden),
        fc1_copy,
        fc2_grad,
        fc2_next,
        fc2_rows_new.reshape(local_hidden),
        row_stats[:, 3],
        fc2_copy,
        norm_grad,
        norm_moment,
        norm_new,
        bias_grad,
        bias_moment,
        bias_new,
        fc1b_grad.reshape(local_hidden),
        fc1b_moment.reshape(local_hidden),
        fc1b_new.reshape(local_hidden),
    )


def solution(mesh):
    in_specs = (
        P("batch", "branch"),
        P("batch", "branch"),
        P("batch", None),
        P("batch", None, "branch"),
        P("branch", "batch"),
        P("batch", "branch"),
        P("branch", "batch"),
        P(),
        P(None, "branch"),
        P("branch"),
        P("batch"),
        P(None, "branch"),
        P("branch"),
        P("batch"),
        P("batch"),
        P("branch"),
        P("branch"),
        P("batch"),
        P(),
        P(None, "branch"),
        P("branch"),
    )
    out_specs = (
        P("batch", "branch"),
        P("batch", "branch"),
        P("batch", None, "branch"),
        P("batch", None, "branch"),
        P("batch"),
        P(None, "branch"),
        P("batch", None, "branch"),
        P("branch", "batch"),
        P("branch", "batch"),
        P("branch"),
        P("batch"),
        P("branch", "batch"),
        P("batch", "branch"),
        P("batch", "branch"),
        P("batch"),
        P("branch"),
        P("batch", "branch"),
        P("branch", "batch"),
        P("branch", "batch"),
        P("branch"),
        P("batch"),
        P("branch", "batch"),
        P(),
        P(),
        P(),
        P(None, "branch"),
        P(None, "branch"),
        P(None, "branch"),
        P("branch"),
        P("branch"),
        P("branch"),
    )
    return jax.shard_map(
        on_device, mesh=mesh, in_specs=in_specs, out_specs=out_specs, check_vma=False
    )
```

profile of v0, /device:TPU:1, one launch (start us, length us, event | category | flops | bytes accessed | tf_op | source)
XLA Modules:
  0.0 604.9 jit_solution(11884128501083106184)
XLA Ops:
  0.7 0.0 copy-start
  0.7 2.1 collective-permute-start
  2.8 1.2 collective-permute-start.1
  4.0 0.0 collective-permute-start.2
  4.1 1.8 copy.97
  5.8 0.9 copy.98
  6.8 1.5 copy.100
  8.3 1.4 copy.101
  9.7 2.4 copy.102
  12.1 1.1 convert_element_type.38
  13.2 1.6 copy.103
  14.8 0.7 convert_element_type.36
  15.5 1.1 copy.99
  16.6 0.0 copy-start.26
  16.7 0.0 copy-start.27
  16.7 0.0 copy-start.28
  16.7 0.0 copy-start.29
  16.7 0.0 copy-start.21
  16.7 0.0 copy-start.22
  16.7 0.0 copy-start.23
  16.7 0.0 copy-start.24
  16.7 0.0 copy-start.25
  16.8 1.9 maximum_maximum_fusion.wst
  18.7 0.6 reshape.171.bias_h
  19.3 0.6 reshape.160.fcb
  19.9 0.6 dynamic_slice.7
  20.5 0.7 copy.106.row_old
  21.2 0.6 reshape.162.f1_old
  21.9 0.6 reshape.163.f2_old
  22.5 0.6 reshape.164.fcb_second
  23.1 0.0 collective-permute-done
  23.1 0.0 collective-permute-done.1
  23.1 0.0 collective-permute-done.2
  23.1 0.8 convert_reduce_fusion
  24.0 3.7 multiply_sine_fusion
  27.7 1.3 broadcast_in_dim.2
  29.0 4.1 concatenate.19.turn_ref
  33.1 510.1 %shard_map.444 = (bf16[6,4,128,512]{3,2,1,0:T(8,128)(2,1)}, bf16[3,3,2,1024,256]{4,3,2,1,0:T(8,128)(2,1)}, f32[3,2,1024,256]{3,2,1,0:T(8,128)}, f32[2,1,384]{2,1...) custom-call(bf16[6,4,128,512]{3,2,1,0:T(8,128)(2,1)} %maximum_maximum_fusion.wst, ...), custom_call_target="tpu_custom_call" | custom-call | flops 80000000000 | bytes 60000000 | tf_op jit(solution)/shard_map/pallas_call | solution.py:814
  543.3 0.0 copy-start.1
  543.3 0.0 copy-start.2
  543.3 0.0 copy-start.4
  543.3 36.4 %shard_map.445 = (bf16[512,1024]{1,0:T(8,128)(2,1)}, bf16[512,1024]{1,0:T(8,128)(2,1)}, f32[128,4]{1,0:T(8,128)}, f32[3,1024]{1,0:T(4,128)}, f32[1,1024]{1,0:T(1...) custom-call(bf16[6,4,128,512]{3,2,1,0:T(8,128)(2,1)} %get-tuple-elem, ...), custom_call_target="tpu_custom_call" | custom-call | flops 50000000 | bytes 40000000 | tf_op jit(solution)/shard_map/pallas_call | solution.py:1303
  579.7 1.3 copy.115
  581.1 1.7 slice_reduce_fusion
  582.8 1.3 copy_bitcast_fusion
  584.2 0.8 copy-done.5
  585.0 0.7 copy-done.6
  585.7 0.7 copy-done.7
  586.4 0.7 copy-done.8
  587.2 0.7 copy-done.9
  587.8 0.7 copy-done.10
  588.5 8.2 %shard_map.446 = (f32[3,128,1024]{2,1,0:T(8,128)}, f32[3,128,1024]{2,1,0:T(8,128)}, bf16[3,128,1024]{2,1,0:T(8,128)(2,1)}, f32[1024,128]{1,0:T(8,128)}, f32[1024...) custom-call(bf16[6,4,128,512]{3,2,1,0:T(8,128)(2,1)} %get-tuple-elem, ...), custom_call_target="tpu_custom_call" | custom-call | flops 20000000 | bytes 30000000 | tf_op jit(solution)/shard_map/pallas_call | solution.py:1412
  596.8 1.0 copy.128
  597.8 1.0 copy.129
  598.7 0.6 copy.130
  599.3 0.6 copy.131
  599.9 0.6 copy.132
  600.5 0.6 copy.133
  601.1 0.6 copy.134
  601.8 0.6 copy.135
  602.4 0.6 copy.136
  603.0 0.6 copy.137
  603.6 0.6 copy.138
  604.2 0.6 copy.139
  (50 shorter events, 0.1 us)
Async XLA Ops:
  0.7 7.6 %copy-start = (f32[128,4096]{1,0:T(8,128)S(1)}, f32[128,4096]{1,0:T(8,128)}, u32[]{:S(2)}) copy-start(f32[128,4096]{1,0:T(8,128)} %w1.3) | copy-start | bytes 6291460
  0.7 22.4 %collective-permute-start = (s32[1,512]{1,0:T(1,128)}, s32[1,512]{1,0:T(1,128)S(1)}, u32[]{:S(2)}, u32[]{:S(2)}) collective-permute-start(s32[1,512]{1,0:T(1,128)} %param.23), channel_id=1, source_target_pairs={{0,2},{2,0},{4,6},{6,4},{8,10},{10,8},{12,14},{14,12},{16,18},{18,... | collective-permute-start | bytes 6152 | tf_op jit(solution)/shard_map/ppermute | solution.py:1497
  2.8 20.3 %collective-permute-start.1 = (s32[1,512]{1,0:T(1,128)}, s32[1,512]{1,0:T(1,128)S(1)}, u32[]{:S(2)}, u32[]{:S(2)}) collective-permute-start(s32[1,512]{1,0:T(1,128)} %param.23), channel_id=1, source_target_pairs={{0,4},{2,6},{4,0},{6,2},{8,12},{10,14},{12,8},{14,10},{16,20},{18,... | collective-permute-start | bytes 6152 | tf_op jit(solution)/shard_map/ppermute | solution.py:1497
  4.0 19.1 %collective-permute-start.2 = (s32[1,512]{1,0:T(1,128)}, s32[1,512]{1,0:T(1,128)S(1)}, u32[]{:S(2)}, u32[]{:S(2)}) collective-permute-start(s32[1,512]{1,0:T(1,128)} %param.23), channel_id=1, source_target_pairs={{0,6},{2,4},{4,2},{6,0},{8,14},{10,12},{12,10},{14,8},{16,22},{18,... | collective-permute-start | bytes 6152 | tf_op jit(solution)/shard_map/ppermute | solution.py:1497
  9.6 2.4 copy-start.11
  12.1 2.7 copy-start.3
  12.1 4.5 slice-start
  13.2 3.5 copy-start.12
  16.6 2.0 copy-start.26
  16.7 2.0 copy-start.27
  16.7 2.0 copy-start.28
  16.7 2.0 copy-start.29
  16.7 2.6 copy-start.21
  16.7 4.5 copy-start.22
  16.7 5.1 copy-start.23
  16.7 5.7 copy-start.24
  16.7 6.4 %copy-start.25 = (s32[1,512]{1,0:T(1,128)S(1)}, s32[1,512]{1,0:T(1,128)}, u32[]{:S(2)}) copy-start(s32[1,512]{1,0:T(1,128)} %param.23) | copy-start | bytes 6148
  543.3 40.9 %copy-start.1 = (f32[128,4096]{1,0:T(8,128)S(1)}, f32[128,4096]{1,0:T(8,128)}, u32[]{:S(2)}) copy-start(f32[128,4096]{1,0:T(8,128)} %w1.3) | copy-start | bytes 6291460
  543.3 40.9 %copy-start.2 = (f32[128,3,1024]{2,0,1:T(8,128)S(1)}, f32[128,3,1024]{2,0,1:T(8,128)}, u32[]{:S(2)}) copy-start(f32[128,3,1024]{2,0,1:T(8,128)} %param.24) | copy-start | bytes 4718596
  543.3 40.9 %copy-start.4 = (f32[1024,128]{1,0:T(8,128)S(1)}, f32[1024,128]{1,0:T(8,128)}, u32[]{:S(2)}) copy-start(f32[1024,128]{1,0:T(8,128)} %wo.3) | copy-start | bytes 1572868
  584.2 0.8 copy-start.5
  585.0 0.7 copy-start.6
  585.7 0.7 copy-start.7
  586.4 0.7 copy-start.8
  587.2 0.7 copy-start.9
  587.8 0.7 copy-start.10
  588.5 8.3 %copy-start.14 = (bf16[512,1024]{1,0:T(8,128)(2,1)S(1)}, bf16[512,1024]{1,0:T(8,128)(2,1)}, u32[]{:S(2)}) copy-start(bf16[512,1024]{1,0:T(8,128)(2,1)} %get-tuple-element.145) | copy-start | bytes 3145732
  588.5 9.2 %copy-start.13 = (bf16[512,1024]{1,0:T(8,128)(2,1)S(1)}, bf16[512,1024]{1,0:T(8,128)(2,1)}, u32[]{:S(2)}) copy-start(bf16[512,1024]{1,0:T(8,128)(2,1)} %get-tuple-element.146) | copy-start | bytes 3145732
  596.7 4.4 copy-start.20
  596.7 5.0 copy-start.19
  596.7 5.6 copy-start.18
  596.7 6.3 %copy-start.17 = (f32[5,1024]{1,0:T(8,128)S(1)}, f32[5,1024]{1,0:T(8,128)}, u32[]{:S(2)}) copy-start(f32[5,1024]{1,0:T(8,128)} %get-tuple-element.170) | copy-start | bytes 61444
  596.8 6.9 %copy-start.16 = (f32[5,1024]{1,0:T(8,128)S(1)}, f32[5,1024]{1,0:T(8,128)}, u32[]{:S(2)}) copy-start(f32[5,1024]{1,0:T(8,128)} %get-tuple-element.171) | copy-start | bytes 61444
  596.8 7.5 %copy-start.15 = (f32[5,1024]{1,0:T(8,128)S(1)}, f32[5,1024]{1,0:T(8,128)}, u32[]{:S(2)}) copy-start(f32[5,1024]{1,0:T(8,128)} %get-tuple-element.172) | copy-start | bytes 61444
where the time goes:
time: 606 us; the launch traced here: 605 us
  Pallas kernels  555 us (92%)
  local copies, waits for them, and re-layouts  37.4 us (6%)
  other arithmetic  8.24 us (1%)
    pallas_call x1, Pallas kernels, block_call(): pl.pallas_call(functools.partial(block_kernel, count), out_shape=[jax.Sha...  510 us
    pallas_call x1, Pallas kernels, tail_call(): pl.pallas_call(functools.partial(tail_kernel, count), out_shape=outs, in_...  36.4 us
    unnamed x77, local copies, waits for them, and re-layouts  17 us
  transfers between devices with their start and end apart: 3, of which 0 were waited for; matrix products, arithmetic and copies ran while one was open for 3% of the time, Pallas kernels for 0%

commit v1 on v0

--- a/solution.py
+++ b/solution.py
@@ -94,7 +94,6 @@
     rsb,
     sib_send,
     sib_land,
-    psend,
     own,
     a2a_s,
     a2a_r,
@@ -320,7 +319,7 @@
         )
 
     def turns_of(rows):
-        table = turn_ref[rows, :]
+        table = turn_ref[:, rows].T
         cos_rows = jnp.where(lane < ROT, table, 1.0)
         sin_rows = pltpu.roll(table, HD - ROT, 1)
         return cos_rows, sin_rows, table[:, 2 * ROT : 2 * ROT + 1]
@@ -443,50 +442,40 @@
         rs_copy(k, way, t).wait_recv()
         return rsb[way, t - 1].astype(jnp.float32)
 
-    def rs_range(low, high):
-        def step(n, carry):
-            k = n // S
-            t = lax.rem(n, S) + 1
-
-            @pl.when((t == 1) & (k >= 1) & (o < outer - 1))
+    def rs_step(k, t):
+        n = k * S + t - 1
+
+        @pl.when((t == 1) & (k >= 1) & (o < outer - 1))
+        def _():
+            pl.semaphore_wait(free_s.at[0], 1)
+
+        @pl.when((t == 1) & (k >= 1) & (o > 0))
+        def _():
+            pl.semaphore_wait(free_s.at[1], 1)
+
+        before = jnp.maximum(n - 1, 0)
+        k_before = before // S
+        t_before = lax.rem(before, S) + 1
+        for way in range(2):
+            owner = o + outer - t if way == 0 else o - outer + t
+
+            @pl.when((n >= 1) & rs_sends(way, t_before))
             def _():
-                pl.semaphore_wait(free_s.at[0], 1)
-
-            @pl.when((t == 1) & (k >= 1) & (o > 0))
+                rs_copy(k_before, way, t_before).wait_send()
+
+            @pl.when(rs_sends(way, t))
             def _():
-                pl.semaphore_wait(free_s.at[1], 1)
-
-            for way in range(2):
-                owner = o + outer - t if way == 0 else o - outer + t
-
-                before = jnp.maximum(n - 1, 0)
-                k_before = before // S
-                t_before = lax.rem(before, S) + 1
-
-                @pl.when((n >= 1) & rs_sends(way, t_before))
+                @pl.when(rs_receives(way, t - 1) & (t > 1))
                 def _():
-                    rs_copy(k_before, way, t_before).wait_send()
-
-                @pl.when(rs_sends(way, t))
+                    sbuf[way] = (
+                        G[lax.rem(k, 2), owner] + rs_fetch(k, way, t - 1)
+                    ).astype(jnp.bfloat16)
+
+                @pl.when(jnp.logical_not(rs_receives(way, t - 1) & (t > 1)))
                 def _():
-                    @pl.when(rs_receives(way, t - 1) & (t > 1))
-                    def _():
-                        sbuf[way] = (
-                            G[lax.rem(k, 2), owner] + rs_fetch(k, way, t - 1)
-                        ).astype(jnp.bfloat16)
-
-                    @pl.when(jnp.logical_not(rs_receives(way, t - 1) & (t > 1)))
-                    def _():
-                        sbuf[way] = G[lax.rem(k, 2), owner].astype(jnp.bfloat16)
-
-                    rs_copy(k, way, t).start()
-
-            return carry
-
-        lax.fori_loop(low, high, step, 0)
-
-    def rs(low, high):
-        rs_range(low * S // 3, high * S // 3)
+                    sbuf[way] = G[lax.rem(k, 2), owner].astype(jnp.bfloat16)
+
+                rs_copy(k, way, t).start()
 
     def gr_copy(k, d, received=False):
         to = near[d - 1]
@@ -541,6 +530,23 @@
         for d in range(1, INNER):
             gr_copy(k, d).start()
         gr_local(k).start()
+
+    def rs_range(low, high):
+        def step(n, carry):
+            k = n // (S + 1)
+            t = lax.rem(n, S + 1) + 1
+
+            @pl.when(t <= S)
+            def _():
+                rs_step(k, t)
+
+            @pl.when(t == S + 1)
+            def _():
+                rs_final(k)
+
+            return carry
+
+        lax.fori_loop(low, high, step, 0)
 
     TILE = T // 2
     TILES = 2 * INNER
@@ -585,18 +591,20 @@
             1 - c,
         )
 
+    def stage(which, i):
+        if which == 0:
+            return H1.at[pl.ds(half, half), pl.ds(pl.multiple_of(i * TILE, 128), TILE)]
+        t = (which - 1) * (TILES - 2) + i
+        return H2.at[
+            pl.ds(pl.multiple_of(t // PER_ROW * half, 128), half),
+            pl.ds(pl.multiple_of(lax.rem(t, PER_ROW) * TILE, 128), TILE),
+        ]
+
     def plane_copy(which, i):
         slot = tile_slot(i)
         low, high = lax.rem(slot, 2), slot // 2
         to = b + low * (1 - 2 * lax.rem(b, 2)) + high * 2 * (1 - 2 * lax.rem(b // 2, 2))
-        if which == 0:
-            src = psend.at[lax.rem(i, 2)]
-        else:
-            t = (which - 1) * (TILES - 2) + i
-            src = H2.at[
-                pl.ds(pl.multiple_of(t // PER_ROW * half, 128), half),
-                pl.ds(pl.multiple_of(lax.rem(t, PER_ROW) * TILE, 128), TILE),
-            ]
+        src = stage(which, i)
         return remote(
             src,
             xr.at[which, slot - 1, lax.rem(i, 2)],
@@ -622,19 +630,7 @@
         @pl.when(i < TILES - 2)
         def _():
             total = (own[...] + sib_land[lax.rem(i, 4)].astype(jnp.float32)).astype(jnp.bfloat16)
-            if which == 0:
-
-                @pl.when(i >= 2)
-                def _():
-                    plane_copy(which, i - 2).wait_send()
-
-                psend[lax.rem(i, 2)] = total
-            else:
-                t = (which - 1) * (TILES - 2) + i
-                H2[
-                    pl.ds(pl.multiple_of(t // PER_ROW * half, 128), half),
-                    pl.ds(pl.multiple_of(lax.rem(t, PER_ROW) * TILE, 128), TILE),
-                ] = total
+            stage(which, i)[...] = total
             plane_copy(which, i).start()
 
         @pl.when(i >= TILES - 2)
@@ -658,43 +654,47 @@
 
         lax.fori_loop(0, TILES, step, 0)
 
-    def sum_sent(which):
+    def sib_sent(which):
         for i in range(TILES - 2, TILES):
             sib_copy(which, i).wait_send()
-        for i in range(TILES - 4, TILES - 2):
-            plane_copy(which, i).wait_send()
-
-    def share(low, high, i, pieces, run):
-        first, last = low * S // 3, high * S // 3
+
+    def spread(first, last, i, pieces, run):
         steps = last - first
         run(
             first + (steps * i + pieces - 1) // pieces,
             first + (steps * (i + 1) + pieces - 1) // pieces,
         )
 
+    def ag_share(low, high, i, pieces):
+        spread(low * S // 3, high * S // 3, i, pieces, ag_range)
+
+    def rs_share(low, high, i, pieces):
+        spread(low * (S + 1) // 4, high * (S + 1) // 4, i, pieces, rs_range)
+
     a2a_start(0)
     gather_one(0, xin, H1)
+    gather_one(1, yin, DY)
+    ag(0, 1)
     a2a_start(1)
-    ag(0, 1)
     gather_two(0, xin, H1)
-    gather_one(1, yin, DY)
+    gather_two(1, yin, DY)
+    ag(1, 2)
     a2a_start(2)
-    ag(1, 2)
     x_local(0, xin, H1).wait()
     sx_wait(0, H1, 0)
     norm_rows(0)
     ag(2, 3)
     gather_three(0, xin, H1)
-    gather_two(1, yin, DY)
+    gather_sent(0, xin, H1)
     for k in range(3, CHUNKS):
         a2a_start(k)
-    gather_sent(0, xin, H1)
     for slot in range(1, INNER):
         sx_wait(0, H1, slot)
         norm_rows(slot)
-        ag(2 + slot, 3 + slot)
-
-    def project_step(h, carry):
+        if slot < 3:
+            ag(2 + slot, 3 + slot)
+
+    def project_step(h):
         ag_wait(h, S)
 
         def slot_step(slot, inner_carry):
@@ -702,12 +702,11 @@
             return inner_carry
 
         lax.fori_loop(0, INNER, slot_step, 0)
-        ag(6 + h, 7 + h)
-        return carry
-
-    project_step(0, 0)
+        ag(5 + h, 6 + h)
+
+    project_step(0)
     gather_three(1, yin, DY)
-    project_step(1, 0)
+    project_step(1)
     x_local(1, yin, DY).wait()
     for slot in range(INNER):
         sx_wait(1, DY, slot)
@@ -716,57 +715,54 @@
     def head_step(h, carry):
         def slot_step(slot, inner_carry):
             head_piece(h, slot)
-            share(8 + 2 * h, 10 + 2 * h, slot, INNER, ag_range)
-            share(0, 3 * h, slot, INNER, rs_range)
+            ag_share(7 + 3 * h, 10 + 3 * h, slot, INNER)
+            rs_share(0, 3 * h, slot, INNER)
             return inner_carry
 
         lax.fori_loop(0, INNER, slot_step, 0)
         grads(h, head_turned(h), H1, 3 * HD)
-
-        @pl.when(h == 1)
-        def _():
-            rs_final(0)
-
         return carry
 
     lax.fori_loop(0, HEADS_DEV, head_step, 0)
+    rs_share(3, 4, 0, 1)
 
     def beside_one(i):
-        share(12, 13, i, TILES, ag_range)
-        share(3, 6, i, TILES, rs_range)
+        ag_share(13, 15, i, TILES)
+        rs_share(4, 7, i, TILES)
 
     sum_tiles(0, beside_one)
 
     def cut_step(f, carry):
         ag_wait(HEADS_DEV + f, S)
 
+        @pl.when(f == CUTS // 2)
+        def _():
+            for i in range(TILES - 2):
+                plane_copy(0, i).wait_send()
+
         def slot_step(slot, inner_carry):
             cut_piece(f, slot)
-            share(
-                jnp.minimum(13 + 2 * f, 18), jnp.minimum(15 + 2 * f, 18), slot, INNER, ag_range
+            ag_share(
+                jnp.minimum(15 + 2 * f, 18), jnp.minimum(17 + 2 * f, 18), slot, INNER
             )
-            share(jnp.maximum(6, 3 + 3 * f), 6 + 3 * f, slot, INNER, rs_range)
+            rs_share(
+                jnp.where(f == 0, 7, 5 + 3 * f),
+                jnp.where(f == 3, 18, 8 + 3 * f),
+                slot,
+                INNER,
+            )
             return inner_carry
 
         lax.fori_loop(0, INNER, slot_step, 0)
         grads(HEADS_DEV + f, cut_turned(f), H2, CUT)
-        rs_final(1 + f)
         return carry
 
     lax.fori_loop(0, CUTS, cut_step, 0)
-    sum_sent(0)
-    sum_tiles(1, lambda i: share(15, 18, i, TILES, rs_range))
-    for i in range(TILES - 2, TILES):
-        sib_copy(1, i).wait_send()
-
-    def beside_last(i):
-        @pl.when(i == 1)
-        def _():
-            rs_final(CHUNKS - 1)
-
-    sum_tiles(2, beside_last)
-    for i in range(TILES - 2, TILES):
-        sib_copy(2, i).wait_send()
+    sib_sent(0)
+    sum_tiles(1, lambda i: rs_share(18, 22, i, TILES))
+    sib_sent(1)
+    sum_tiles(2, lambda i: rs_share(22, 24, i, TILES))
+    sib_sent(2)
 
     gr_sent(CHUNKS - 1)
 
@@ -836,7 +832,6 @@
             pltpu.VMEM((2, S, WIDE, INNER * rows), low),
             pltpu.VMEM((2, half, tile), low),
             pltpu.VMEM((4, half, tile), low),
-            pltpu.VMEM((2, half, tile), low),
             pltpu.VMEM((half, tile), high),
             dma((CHUNKS, INNER - 1)),
             dma((CHUNKS, INNER - 1)),
@@ -1117,7 +1112,9 @@
         ).astype(jnp.bfloat16)
     pair_copy(rsum, rsum_in, 1).wait_recv()
     rows_after = renew_stat(row_old[...], (rsum[...] + rsum_in[...])[:, :4])
-    row_new[...] = rows_after
+    row_new[...] = jnp.concatenate(
+        [rows_after, jnp.zeros((R, 128 - 4), jnp.float32)], axis=1
+    )
 
     chain_waits(pay, z_in, 0)
     acc = z_in[0]
@@ -1283,7 +1280,7 @@
     outs = [
         out(tokens, half, dtype=jnp.bfloat16),
         out(tokens, half, dtype=jnp.bfloat16),
-        out(rows, 4),
+        out(rows, 128),
         out(3, half),
         out(1, half),
         out(INNER, 1, half),
@@ -1340,32 +1337,24 @@
     )(*args)
 
 
-def update_kernel(
-    gr,
-    wq,
-    wo,
-    w1,
-    w2,
-    row_new,
-    qc_new,
-    or_new,
-    f1_new,
-    f2_new,
-    coef,
-    q_grad,
-    q_next,
-    q_copy,
-    o_grad,
-    o_next,
-    o_copy,
-    f1_grad,
-    f1_next,
-    f1_copy,
-    f2_grad,
-    f2_next,
-    f2_copy,
-):
-    side = lax.rsqrt(row_new[...]) * coef[0:1, :4]
+def update_kernel(*refs):
+    gr, wq, wo, w1, w2, row_new, coef = refs[:7]
+    small = refs[7:22]
+    qc_new, or_new, f1_new, f2_new = small[2:6]
+    q_grad, q_next, q_copy, o_grad, o_next, o_copy = refs[22:28]
+    f1_grad, f1_next, f1_copy, f2_grad, f2_next, f2_copy = refs[28:34]
+    row_out, small_out = refs[34:38], refs[38:]
+    part = pl.program_id(0)
+    side = lax.rsqrt(row_new[:, :4]) * coef[0:1, :4]
+    width_q = HEADS_DEV * HD
+
+    @pl.when(part == 0)
+    def _():
+        for source, target in zip(small, small_out):
+            target[...] = source[...]
+        turned = row_new[...].T
+        for place in range(4):
+            row_out[place][...] = turned[place : place + 1, :]
 
     def put(grad_ref, next_ref, copy_ref, where, weight, gradient, update):
         fresh = weight[where] - update
@@ -1375,27 +1364,28 @@
 
     for h in range(HEADS_DEV):
         gradient = gr[h, 0].astype(jnp.float32)
+        cols = pl.ds(pl.multiple_of(part * width_q + h * HD, HD), HD)
         for p in range(3):
             mine = gradient[:, p * HD : (p + 1) * HD]
-            update = mine * side[:, 0:1] * lax.rsqrt(qc_new[p : p + 1, h * HD : (h + 1) * HD])
+            update = mine * side[:, 0:1] * lax.rsqrt(qc_new[p : p + 1, cols])
             where = (p, slice(None), slice(h * HD, (h + 1) * HD))
             put(q_grad, q_next, q_copy, where, wq, mine, update)
         mine = gradient[:, 3 * HD :]
-        update = mine * side[:, 2:3] * lax.rsqrt(or_new[:, h * HD : (h + 1) * HD])
+        update = mine * side[:, 2:3] * lax.rsqrt(or_new[:, cols])
         where = (slice(h * HD, (h + 1) * HD), slice(None))
         put(o_grad, o_next, o_copy, where, wo, mine.T, update.T)
     for f in range(CUTS):
         gradient = gr[HEADS_DEV + f, 0].astype(jnp.float32)
         cols = slice(f * CUT, (f + 1) * CUT)
         mine = gradient[:, :CUT]
-        update = mine * side[:, 1:2] * lax.rsqrt(f1_new[0, :, cols])
+        update = mine * side[:, 1:2] * lax.rsqrt(f1_new[part, :, cols])
         put(f1_grad, f1_next, f1_copy, (slice(None), cols), w1, mine, update)
         mine = gradient[:, CUT:]
-        update = mine * side[:, 3:4] * lax.rsqrt(f2_new[0, :, cols])
+        update = mine * side[:, 3:4] * lax.rsqrt(f2_new[part, :, cols])
         put(f2_grad, f2_next, f2_copy, (cols, slice(None)), w2, mine.T, update.T)
 
 
-def update_call(gr, wq, wo, w1, w2, row_new, qc_new, or_new, f1_new, f2_new, coef):
+def update_call(gr, wq, wo, w1, w2, row_new, coef, *small):
     rows = gr.shape[2]
     width_q = HEADS_DEV * HD
     hidden_q = CUTS * CUT
@@ -1409,6 +1399,16 @@
         for dtype in (jnp.float32, jnp.float32, jnp.bfloat16):
             outs.append(jax.ShapeDtypeStruct(array.shape, dtype))
             out_specs.append(its)
+
+    def fixed(shape):
+        return spec(shape, lambda i: (0,) * len(shape))
+
+    for _ in range(4):
+        outs.append(jax.ShapeDtypeStruct((1, rows), jnp.float32))
+        out_specs.append(fixed((1, rows)))
+    for array in small:
+        outs.append(jax.ShapeDtypeStruct(array.shape, array.dtype))
+        out_specs.append(fixed(array.shape))
     return pl.pallas_call(
         update_kernel,
         grid=(INNER,),
@@ -1419,19 +1419,16 @@
             o_spec,
             f1_spec,
             f2_spec,
-            spec((rows, 4), lambda i: (0, 0)),
-            spec((3, width_q), lambda i: (0, i)),
-            spec((1, width_q), lambda i: (0, i)),
-            spec((1, 1, hidden_q), lambda i: (i, 0, 0)),
-            spec((1, 1, hidden_q), lambda i: (i, 0, 0)),
-            spec((8, 128), lambda i: (0, 0)),
-        ],
+            fixed((rows, 128)),
+            fixed((8, 128)),
+        ]
+        + [fixed(array.shape) for array in small],
         out_specs=out_specs,
         compiler_params=pltpu.CompilerParams(vmem_limit_bytes=48 * 1024 * 1024),
         cost_estimate=pl.CostEstimate(
             flops=20_000_000, bytes_accessed=30_000_000, transcendentals=100_000
         ),
-    )(gr, wq, wo, w1, w2, row_new, qc_new, or_new, f1_new, f2_new, coef)
+    )(gr, wq, wo, w1, w2, row_new, coef, *small)
 
 
 def swap_pairs(count, step):
@@ -1499,15 +1496,21 @@
     )
     positions_idx = jnp.arange(tokens)
     earlier = jnp.sum((segment[:, None, :] < segment[:, :, None]).astype(jnp.int32), axis=2)
-    starts = earlier.astype(jnp.float32).reshape(group, 1)
-    places = (positions_idx[None] - earlier).astype(jnp.float32).reshape(group, 1)
+    starts = earlier.astype(jnp.float32).reshape(1, group)
+    places = (positions_idx[None] - earlier).astype(jnp.float32).reshape(1, group)
     frequency = 10000.0 ** (-2.0 * jnp.arange(ROT // 2, dtype=jnp.float32) / ROT)
-    angles = places * frequency[None, :]
+    angles = frequency[:, None] * places
     cos_part = jnp.cos(angles)
     sin_part = jnp.sin(angles)
-    rest = (group, HD - 2 * ROT)
     turns = jnp.concatenate(
-        [cos_part, cos_part, -sin_part, sin_part, jnp.broadcast_to(starts, rest)], axis=1
+        [
+            cos_part,
+            cos_part,
+            -sin_part,
+            sin_part,
+            jnp.broadcast_to(starts, (HD - 2 * ROT, group)),
+        ],
+        axis=0,
     )
     bias_h = (
         block_of(proj_bias[0:3], q, width_q, 1)
@@ -1566,45 +1569,72 @@
         head_bias,
         cut_bias,
     )
-    updated = update_call(
-        received,
-        qkv_parts,
-        w_out,
-        w_fc1,
-        w_fc2,
-        row_stats,
+    small = (
+        output,
+        input_grad,
         qkv_cols_new,
         out_rows_new,
         fc1_cols_new,
         fc2_rows_new,
-        factors,
+        norm_grad,
+        norm_moment,
+        norm_new,
+        bias_grad,
+        bias_moment,
+        bias_new,
+        fc1b_grad,
+        fc1b_moment,
+        fc1b_new,
+    )
+    updated = update_call(
+        received, qkv_parts, w_out, w_fc1, w_fc2, row_stats, factors, *small
     )
     qkv_grad, qkv_next, qkv_copy = (array.transpose(1, 0, 2) for array in updated[0:3])
     out_grad, out_next, out_copy = updated[3:6]
     fc1_grad, fc1_next, fc1_copy = updated[6:9]
     fc2_grad, fc2_next, fc2_copy = updated[9:12]
+    qkv_rows_new, fc1_rows_new, out_cols_new, fc2_cols_new = (
+        array.reshape(rows) for array in updated[12:16]
+    )
+    (
+        output,
+        input_grad,
+        qkv_cols_new,
+        out_rows_new,
+        fc1_cols_new,
+        fc2_rows_new,
+        norm_grad,
+        norm_moment,
+        norm_new,
+        bias_grad,
+        bias_moment,
+        bias_new,
+        fc1b_grad,
+        fc1b_moment,
+        fc1b_new,
+    ) = updated[16:]
     return (
         output,
         input_grad,
         qkv_grad,
         qkv_next,
-        row_stats[:, 0],
+        qkv_rows_new,
         qkv_cols_new,
         qkv_copy,
         out_grad,
         out_next,
         out_rows_new.reshape(local_width),
-        row_stats[:, 2],
+        out_cols_new,
         out_copy,
         fc1_grad,
         fc1_next,
-        row_stats[:, 1],
+        fc1_rows_new,
         fc1_cols_new.reshape(local_hidden),
         fc1_copy,
         fc2_grad,
         fc2_next,
         fc2_rows_new.reshape(local_hidden),
-        row_stats[:, 3],
+        fc2_cols_new,
         fc2_copy,
         norm_grad,
         norm_moment,

time: 606 us -> 560 us (0.924)
  Pallas kernels: 555 us -> 520 us
  local copies, waits for them, and re-layouts: 37.4 us -> 27.1 us
    pallas_call x1, Pallas kernels: 510 us -> 470 us  [block_call(): pl.pallas_call(functools.partial(block_kernel, count), out_shape=[jax.Sha...]
    unnamed x77 -> x65, local copies, waits for them, and re-layouts: 17 us -> 18.7 us
where the time goes in v1:
time: 560 us; the launch traced here: 558 us
  Pallas kernels  520 us (93%)
  local copies, waits for them, and re-layouts  27.1 us (5%)
  other arithmetic  7.06 us (1%)
    pallas_call x1, Pallas kernels, block_call(): pl.pallas_call(functools.partial(block_kernel, count), out_shape=[jax.Sha...  470 us
    pallas_call x1, Pallas kernels, tail_call(): pl.pallas_call(functools.partial(tail_kernel, count), out_shape=outs, in_...  40.5 us
    unnamed x65, local copies, waits for them, and re-layouts  18.7 us
  transfers between devices with their start and end apart: 3, of which 0 were waited for; matrix products, arithmetic and copies ran while one was open for 3% of the time, Pallas kernels for 0%

profile of v1, /device:TPU:1, one launch (start us, length us, event | category | flops | bytes accessed | tf_op | source)
XLA Modules:
  0.0 558.5 jit_solution(3572507560247503783)
XLA Ops:
  0.7 2.1 collective-permute-start.1
  2.8 1.2 collective-permute-start
  4.0 0.1 collective-permute-start.2
  4.1 1.1 convert_element_type.36
  5.1 0.2 copy.90
  5.3 1.8 copy.88
  7.1 0.1 copy.89
  7.2 0.0 copy-start.19
  7.2 1.2 copy.91
  8.4 1.8 copy.92
  10.2 1.3 copy.93
  11.5 0.0 copy-start.28
  11.5 0.0 copy-start.29
  11.6 0.1 convert_element_type.38
  11.7 0.5 copy.94
  12.2 0.0 slice-done
  12.3 0.0 copy-start.20
  12.3 0.0 copy-start.22
  12.3 0.0 copy-start.23
  12.3 0.0 copy-start.24
  12.3 0.0 copy-start.25
  12.4 3.0 maximum_maximum_fusion.wst
  15.4 0.6 reshape.172.fcb
  16.1 0.6 dynamic_slice.7
  16.6 0.6 reshape.174.f1_old
  17.3 0.0 copy-done.23
  17.3 0.6 reshape.175.f2_old
  17.9 0.6 reshape.176.fcb_second
  18.5 0.6 reshape.187.bias_h
  19.1 0.7 copy.96.row_old
  19.8 0.0 collective-permute-done.1
  19.8 0.0 collective-permute-done
  19.8 0.0 collective-permute-done.2
  19.9 0.8 convert_reduce_fusion
  20.7 0.5 fusion
  21.2 0.5 fusion.1
  21.7 0.5 fusion.4
  22.2 0.5 fusion.2
  22.8 0.0 copy-start.21
  22.8 1.0 copy-done.21
  23.8 469.5 %shard_map.444 = (bf16[6,4,128,512]{3,2,1,0:T(8,128)(2,1)}, bf16[3,3,2,1024,256]{4,3,2,1,0:T(8,128)(2,1)}, f32[3,2,1024,256]{3,2,1,0:T(8,128)}, f32[2,1,384]{2,1...) custom-call(bf16[6,4,128,512]{3,2,1,0:T(8,128)(2,1)} %maximum_maximum_fusion.wst, ...), custom_call_target="tpu_custom_call" | custom-call | flops 80000000000 | bytes 60000000 | tf_op jit(solution)/shard_map/pallas_call | solution.py:810
  493.3 0.0 copy-start
  493.3 0.0 copy-start.1
  493.3 40.5 %shard_map.445 = (bf16[512,1024]{1,0:T(8,128)(2,1)}, bf16[512,1024]{1,0:T(8,128)(2,1)}, f32[128,128]{1,0:T(8,128)}, f32[3,1024]{1,0:T(4,128)}, f32[1,1024]{1,0:T...) custom-call(bf16[6,4,128,512]{3,2,1,0:T(8,128)(2,1)} %get-tuple-elem, ...), custom_call_target="tpu_custom_call" | custom-call | flops 50000000 | bytes 40000000 | tf_op jit(solution)/shard_map/pallas_call | solution.py:1300
  533.8 1.2 copy-done.2
  535.0 1.2 copy-done.3
  536.3 0.8 copy-done.4
  537.1 0.8 copy-done.5
  537.9 0.8 copy-done.6
  538.6 0.8 copy-done.7
  539.4 0.8 copy-done.8
  540.1 0.8 copy-done.9
  540.9 0.8 copy-done.10
  541.7 0.7 copy-done.11
  542.4 0.7 copy-done.12
  543.1 0.7 copy-done.13
  543.8 0.7 copy-done.14
  544.5 0.7 copy-done.15
  545.2 0.7 copy-done.16
  546.0 0.7 copy-done.17
  546.6 0.7 copy-done.18
  547.3 9.9 %shard_map.446 = (f32[3,128,1024]{2,1,0:T(8,128)}, f32[3,128,1024]{2,1,0:T(8,128)}, bf16[3,128,1024]{2,1,0:T(8,128)(2,1)}, f32[1024,128]{1,0:T(8,128)}, f32[1024...) custom-call(bf16[6,4,128,512]{3,2,1,0:T(8,128)(2,1)} %get-tuple-elem, ...), custom_call_target="tpu_custom_call" | custom-call | flops 20000000 | bytes 30000000 | tf_op jit(solution)/shard_map/pallas_call | solution.py:1412
  557.2 0.6 copy.105
  557.8 0.6 copy_bitcast_fusion
  (39 shorter events, 0.1 us)
Async XLA Ops:
  0.7 19.2 %collective-permute-start.1 = (s32[1,512]{1,0:T(1,128)}, s32[1,512]{1,0:T(1,128)S(1)}, u32[]{:S(2)}, u32[]{:S(2)}) collective-permute-start(s32[1,512]{1,0:T(1,128)} %param.23), channel_id=1, source_target_pairs={{0,4},{2,6},{4,0},{6,2},{8,12},{10,14},{12,8},{14,10},{16,20},{18,... | collective-permute-start | bytes 6152 | tf_op jit(solution)/shard_map/ppermute | solution.py:1494
  2.8 17.0 %collective-permute-start = (s32[1,512]{1,0:T(1,128)}, s32[1,512]{1,0:T(1,128)S(1)}, u32[]{:S(2)}, u32[]{:S(2)}) collective-permute-start(s32[1,512]{1,0:T(1,128)} %param.23), channel_id=1, source_target_pairs={{0,2},{2,0},{4,6},{6,4},{8,10},{10,8},{12,14},{14,12},{16,18},{18,... | collective-permute-start | bytes 6152 | tf_op jit(solution)/shard_map/ppermute | solution.py:1494
  4.0 15.8 %collective-permute-start.2 = (s32[1,512]{1,0:T(1,128)}, s32[1,512]{1,0:T(1,128)S(1)}, u32[]{:S(2)}, u32[]{:S(2)}) collective-permute-start(s32[1,512]{1,0:T(1,128)} %param.23), channel_id=1, source_target_pairs={{0,6},{2,4},{4,2},{6,0},{8,14},{10,12},{12,10},{14,8},{16,22},{18,... | collective-permute-start | bytes 6152 | tf_op jit(solution)/shard_map/ppermute | solution.py:1494
  7.2 4.3 copy-start.19
  11.5 0.7 slice-start
  11.5 0.7 copy-start.26
  11.5 0.7 copy-start.27
  11.5 0.7 copy-start.28
  11.5 0.7 copy-start.29
  12.3 3.1 copy-start.20
  12.3 4.3 copy-start.22
  12.3 4.9 copy-start.23
  12.3 5.5 copy-start.24
  12.3 7.5 %copy-start.25 = (s32[1,512]{1,0:T(1,128)S(1)}, s32[1,512]{1,0:T(1,128)}, u32[]{:S(2)}) copy-start(s32[1,512]{1,0:T(1,128)} %param.23) | copy-start | bytes 6148
  22.8 1.0 copy-start.21
  493.3 40.5 %copy-start = (f32[128,3,1024]{2,0,1:T(8,128)S(1)}, f32[128,3,1024]{2,0,1:T(8,128)}, u32[]{:S(2)}) copy-start(f32[128,3,1024]{2,0,1:T(8,128)} %param.24) | copy-start | bytes 4718596
  493.3 40.5 %copy-start.1 = (f32[1024,128]{1,0:T(8,128)S(1)}, f32[1024,128]{1,0:T(8,128)}, u32[]{:S(2)}) copy-start(f32[1024,128]{1,0:T(8,128)} %refs_2_.1) | copy-start | bytes 1572868
  533.8 1.2 copy-start.2
  535.0 1.2 copy-start.3
  536.3 0.8 copy-start.4
  537.1 0.8 copy-start.5
  537.9 0.8 copy-start.6
  538.6 0.8 copy-start.7
  539.4 0.8 copy-start.8
  540.1 0.8 copy-start.9
  540.9 0.8 copy-start.10
  541.7 0.7 copy-start.11
  542.4 0.7 copy-start.12
  543.1 0.7 copy-start.13
  543.8 0.7 copy-start.14
  544.5 0.7 copy-start.15
  545.2 0.7 copy-start.16
  546.0 0.7 copy-start.17
  546.6 0.7 copy-start.18
